TPU v7x, 128 devices: a whole 4x4x4 slice. The times are simulated.
128 devices in a mesh: fsdp: 32 (over y, x, core), tp: 4 (over z).
Axes of the slice: x: 4, y: 4, z: 4, core: 2. Of those that a mesh axis runs over, the one named last changes fastest.
Arguments:
- roll_rows: bfloat16 [1024, 72, 3584], P('fsdp', None, 'tp'), may hold values from -60 to 60
- dest: int32 [1024], P('fsdp'), may hold values from 0 to 1023, as said below
- lengths: int32 [32, 32], P('fsdp'), may hold values from 1 to 72, 768 in all within a row
- clusters: int32 [1024], P('fsdp'), may hold values from 0 to 3
- log_prob_grad: bfloat16 [24576, 3584], P('fsdp', 'tp'), may hold values from -6 to 6
- gain: bfloat16 [3584], replicated, may hold values from 0.5 to 1.5
- w_q: bfloat16 [3584, 2048], P('fsdp', 'tp'), may hold values from -1 to 1
- w_k: bfloat16 [3584, 512], P('fsdp', 'tp'), may hold values from -1 to 1
- w_v: bfloat16 [3584, 512], P('fsdp', 'tp'), may hold values from -0.09375 to 0.09375
- w_o_t: bfloat16 [3584, 2048], P('fsdp', 'tp'), may hold values from -0.125 to 0.125
Outputs:
- input_grad: bfloat16 [24576, 3584], P('fsdp', 'tp')
- grad_q: bfloat16 [3584, 2048], P('fsdp', 'tp')
- grad_k: bfloat16 [3584, 512], P('fsdp', 'tp')
- grad_v: bfloat16 [3584, 512], P('fsdp', 'tp')
- grad_o_t: bfloat16 [3584, 2048], P('fsdp', 'tp')
Inputs may be any that keep to these rules, and one draw needn't show every extreme that they name: dest is a permutation; every rollout replica hands exactly 1 completions to every learner, and every learner trains 32 completions. Each learner's 32 lengths sum to 768.
All inputs are finite; a program needn't handle non-finite values.
Results may differ from a plain program's by a relative error of at most 0.03.
Values may be sent and summed in bfloat16 or wider, within the bound.
A program may use at most 128 MiB of HBM per device.

v0:
```python
import jax
import jax.numpy as jnp
from jax import lax
from jax.sharding import PartitionSpec as P

KEY_VALUE_HEADS = 4
HD = 128
QUERY_HEADS = 16
GSIZE = 16


ROPE_BASE = 1000000.0
NORM_EPSILON = 1e-06


def contract_rows(left, right):
    return lax.dot_general(
        left, right, (((0,), (0,)), ((), ())), preferred_element_type=jnp.float32
    )


def times_trans(left, right):
    return lax.dot_general(
        left, right, (((1,), (1,)), ((), ())), preferred_element_type=jnp.float32
    )


def rotary_tables(position):
    half_width = HD // 2
    frequency = ROPE_BASE ** (-(2.0 * jnp.arange(half_width, dtype=jnp.float32)) / HD)
    angles = position.astype(jnp.float32)[:, None] * frequency[None, :]
    return (jnp.cos(angles)[:, None, :], jnp.sin(angles)[:, None, :])


def rotate(values, rope_cos, rope_sin):
    half_width = values.shape[-1] // 2
    first_half = values[..., :half_width]
    second_half = values[..., half_width:]
    return jnp.concatenate(
        [
            first_half * rope_cos - second_half * rope_sin,
            second_half * rope_cos + first_half * rope_sin,
        ],
        axis=-1,
    )


def inverse_rotate(values, rope_cos, rope_sin):
    half_width = values.shape[-1] // 2
    first_half = values[..., :half_width]
    second_half = values[..., half_width:]
    return jnp.concatenate(
        [
            first_half * rope_cos + second_half * rope_sin,
            second_half * rope_cos - first_half * rope_sin,
        ],
        axis=-1,
    )


def per_device(roll_rows, dest, lengths, clusters, log_prob_grad, gain, w_q, w_k, w_v, w_o_t):
    sequence_count = dest.shape[0]
    max_len = roll_rows.shape[1]
    local_features = roll_rows.shape[2]
    per_pair = sequence_count // lax.axis_size("fsdp")
    slot_ids = jnp.arange(sequence_count, dtype=jnp.int32)
    target = dest // sequence_count
    within = dest % sequence_count
    ballots = clusters.reshape(sequence_count // GSIZE, GSIZE)
    vote_share = jnp.mean((ballots[:, :, None] == ballots[:, None, :]).astype(jnp.float32), axis=2)
    advantage = (
        (vote_share - jnp.mean(vote_share, axis=1, keepdims=True))
        .reshape(sequence_count)
        .astype(jnp.bfloat16)
    )
    same_target = target[:, None] == target[None, :]
    earlier = within[None, :] < within[:, None]
    rank_in = jnp.sum((same_target & earlier).astype(jnp.int32), axis=1)
    send_block = target * per_pair + rank_in
    source = jnp.sum(
        jnp.where(send_block[None, :] == slot_ids[:, None], slot_ids[None, :], 0), axis=1
    )
    send_rows = jnp.take(roll_rows, source, axis=0)
    send_place = jnp.take(within, source).astype(jnp.bfloat16)
    send_share = jnp.take(advantage, source)
    arrived_rows, arrived_place, arrived_share = (
        lax.all_to_all(send_rows, "fsdp", split_axis=0, concat_axis=0, tiled=True),
        lax.all_to_all(send_place, "fsdp", split_axis=0, concat_axis=0, tiled=True),
        lax.all_to_all(send_share, "fsdp", split_axis=0, concat_axis=0, tiled=True),
    )
    lengths_row = lengths.reshape(sequence_count)
    sequence_ends = jnp.cumsum(lengths_row)
    sequence_starts = sequence_ends - lengths_row
    row_count = log_prob_grad.shape[0]
    row_index = jnp.arange(row_count, dtype=jnp.int32)
    segment = jnp.sum((sequence_ends[None, :] <= row_index[:, None]).astype(jnp.int32), axis=1)
    one_hot = segment[:, None] == slot_ids[None, :]
    position = row_index - jnp.sum(jnp.where(one_hot, sequence_starts[None, :], 0), axis=1)
    holder = arrived_place.astype(jnp.int32)[None, :] == slot_ids[:, None]
    slot_of = jnp.sum(jnp.where(holder, slot_ids[None, :], 0), axis=1)
    seq_advantage = jnp.sum(
        jnp.where(holder, arrived_share.astype(jnp.float32)[None, :], 0.0), axis=1
    )
    row_slot = jnp.sum(jnp.where(one_hot, slot_of[None, :], 0), axis=1)
    row_advantage = jnp.sum(jnp.where(one_hot, seq_advantage[None, :], 0.0), axis=1)
    learner_rows = jnp.take(
        arrived_rows.reshape(sequence_count * max_len, local_features),
        row_slot * max_len + position,
        axis=0,
    )
    packed, cotangent = (
        lax.all_gather(learner_rows, "tp", axis=1, tiled=True),
        lax.all_gather(log_prob_grad, "tp", axis=1, tiled=True),
    )
    inputs_float = packed.astype(jnp.float32)
    inverse_norm = lax.rsqrt(
        jnp.mean(inputs_float * inputs_float, axis=1, keepdims=True) + NORM_EPSILON
    )
    unit_rows = inputs_float * inverse_norm
    gain_float = gain.astype(jnp.float32)
    normed = (unit_rows * gain_float).astype(jnp.bfloat16)
    rope_cos, rope_sin = rotary_tables(position)
    allowed = (segment[:, None] == segment[None, :]) & (position[None, :] <= position[:, None])
    grad_local = row_advantage[:, None] * log_prob_grad.astype(jnp.float32)
    grad_round = (row_advantage[:, None] * cotangent.astype(jnp.float32)).astype(jnp.bfloat16)
    weight_q, weight_k, weight_v, weight_o = (
        lax.all_gather(w_q, "fsdp", axis=0, tiled=True),
        lax.all_gather(w_k, "fsdp", axis=0, tiled=True),
        lax.all_gather(w_v, "fsdp", axis=0, tiled=True),
        lax.all_gather(w_o_t, "fsdp", axis=0, tiled=True),
    )
    query_lin = jnp.dot(normed, weight_q, preferred_element_type=jnp.float32)
    key_lin = jnp.dot(normed, weight_k, preferred_element_type=jnp.float32)
    value_lin = jnp.dot(normed, weight_v, preferred_element_type=jnp.float32)
    key_heads = w_k.shape[1] // HD
    queries_per_group = QUERY_HEADS // KEY_VALUE_HEADS
    query_rot = (
        rotate(query_lin.reshape(row_count, key_heads * queries_per_group, HD), rope_cos, rope_sin)
        .astype(jnp.bfloat16)
        .reshape(row_count, key_heads, queries_per_group, HD)
    )
    key_rot = rotate(key_lin.reshape(row_count, key_heads, HD), rope_cos, rope_sin).astype(
        jnp.bfloat16
    )
    value_b = value_lin.reshape(row_count, key_heads, HD).astype(jnp.bfloat16)
    scores = jnp.einsum(
        "ighd,jgd->ghij", query_rot, key_rot, preferred_element_type=jnp.float32
    ) * HD ** (-0.5)
    scores = jnp.where(allowed, scores, -1e30)
    row_max = jnp.max(scores, axis=-1, keepdims=True)
    exp_scores = jnp.where(allowed, jnp.exp(scores - row_max), 0.0)
    attn_prob = exp_scores / jnp.sum(exp_scores, axis=-1, keepdims=True)
    attn_prob_b = attn_prob.astype(jnp.bfloat16)
    attn_out = jnp.einsum(
        "ghij,jgd->ighd", attn_prob_b, value_b, preferred_element_type=jnp.float32
    )
    attn_out = attn_out.reshape(row_count, key_heads * queries_per_group * HD).astype(jnp.bfloat16)
    grad_attn = jnp.dot(grad_round, weight_o, preferred_element_type=jnp.float32).astype(
        jnp.bfloat16
    )
    grad_attn = grad_attn.reshape(row_count, key_heads, queries_per_group, HD)
    grad_prob = jnp.einsum("ighd,jgd->ghij", grad_attn, value_b, preferred_element_type=jnp.float32)
    grad_value_f = jnp.einsum(
        "ghij,ighd->jgd", attn_prob_b, grad_attn, preferred_element_type=jnp.float32
    )
    row_delta = jnp.sum(attn_prob * grad_prob, axis=-1, keepdims=True)
    grad_score = (attn_prob * (grad_prob - row_delta) * HD ** (-0.5)).astype(jnp.bfloat16)
    grad_qrot = jnp.einsum(
        "ghij,jgd->ighd", grad_score, key_rot, preferred_element_type=jnp.float32
    )
    grad_qrot = grad_qrot.reshape(row_count, key_heads * queries_per_group, HD)
    grad_krot = jnp.einsum(
        "ghij,ighd->jgd", grad_score, query_rot, preferred_element_type=jnp.float32
    )
    grad_query = (
        inverse_rotate(grad_qrot, rope_cos, rope_sin).astype(jnp.bfloat16).reshape(row_count, -1)
    )
    grad_key = (
        inverse_rotate(grad_krot, rope_cos, rope_sin).astype(jnp.bfloat16).reshape(row_count, -1)
    )
    grad_value = grad_value_f.astype(jnp.bfloat16).reshape(row_count, -1)
    grad_normed = (
        times_trans(grad_query, weight_q)
        + times_trans(grad_key, weight_k)
        + times_trans(grad_value, weight_v)
    )
    grad_hat = grad_normed * gain_float
    grad_in = inverse_norm * (
        grad_hat - unit_rows * jnp.mean(grad_hat * unit_rows, axis=1, keepdims=True)
    )
    summed_in = lax.psum_scatter(
        grad_in.astype(jnp.bfloat16), "tp", scatter_dimension=1, tiled=True
    ).astype(jnp.float32)
    input_grad = (grad_local + summed_in).astype(jnp.bfloat16)
    summed = lax.psum_scatter(
        jnp.concatenate(
            [
                contract_rows(normed, grad_query),
                contract_rows(normed, grad_key),
                contract_rows(normed, grad_value),
                contract_rows(grad_round, attn_out),
            ],
            axis=1,
        ).astype(jnp.bfloat16),
        "fsdp",
        scatter_dimension=0,
        tiled=True,
    ).astype(jnp.float32)
    q_cols = w_q.shape[1]
    k_cols = w_k.shape[1]
    grad_q = summed[:, :q_cols].astype(jnp.bfloat16)
    grad_k = summed[:, q_cols : q_cols + k_cols].astype(jnp.bfloat16)
    grad_v = summed[:, q_cols + k_cols : q_cols + 2 * k_cols].astype(jnp.bfloat16)
    grad_o_t = summed[:, q_cols + 2 * k_cols :].astype(jnp.bfloat16)
    return (input_grad, grad_q, grad_k, grad_v, grad_o_t)


def solution(mesh):
    in_specs = (
        P("fsdp", None, "tp"),
        P("fsdp"),
        P("fsdp", None),
        P("fsdp"),
        P("fsdp", "tp"),
        P(),
        P("fsdp", "tp"),
        P("fsdp", "tp"),
        P("fsdp", "tp"),
        P("fsdp", "tp"),
    )
    out_specs = (
        P("fsdp", "tp"),
        P("fsdp", "tp"),
        P("fsdp", "tp"),
        P("fsdp", "tp"),
        P("fsdp", "tp"),
    )
    return jax.shard_map(
        per_device, mesh=mesh, in_specs=in_specs, out_specs=out_specs, check_vma=False
    )
```

profile of v0, /device:TPU:1, one launch (start us, length us, event | category | flops | bytes accessed | tf_op | source)
XLA Modules:
  0.0 508.6 jit_solution(12253574929329745245)
XLA Ops:
  11.1 8.6 %all-to-all-start = ((bf16[32,1,1]{2,1,0:T(2,128)(2,1)}), bf16[32,1,1]{2,1,0:T(2,128)(2,1)S(1)}, u32[]{:S(2)}, u32[]{:S(2)}) async-start(bf16[32,1,1]{2,1,0:T(2,128)(2,1)} %copy.87), calls=%async_computation | async-start | bytes 32768 | tf_op jit(solution)/shard_map/all_to_all | solution.py:88
  19.7 5.2 %gather_fusion.2 = bf16[32,72,896]{2,1,0:T(8,128)(2,1)} fusion(bf16[32,72,896]{2,1,0:T(8,128)(2,1)} %param.10, s32[1024]{0:T(1024)S(1)} %pad_clamp_fusion.1), kind=kCustom, calls=%fused_computation.2 | custom fusion | bytes 8257664 | tf_op jit(solution)/shard_map/jit(_take)/gather | solution.py:83
  24.9 4.6 broadcast_select_fusion
  29.5 7.6 %all-to-all-start.2 = ((bf16[32,72,896]{2,1,0:T(8,128)(2,1)}), bf16[32,72,896]{2,1,0:T(8,128)(2,1)}, u32[]{:S(2)}, u32[]{:S(2)}) async-start(bf16[32,72,896]{2,1,0:T(8,128)(2,1)} %broadcast_select_fusion), calls=%async_computation.2 | async-start | bytes 8257536 | tf_op jit(solution)/shard_map/all_to_all | solution.py:87
  38.4 54.6 %all-to-all-done.2 = bf16[32,72,896]{2,1,0:T(8,128)(2,1)} async-done(((bf16[32,72,896]{2,1,0:T(8,128)(2,1)}), bf16[32,72,896]{2,1,0:T(8,128)(2,1)}, u32[]{:S(2)}, u32[]{:S(2)}) %all-to-all-start.2) | async-done | bytes 4128800 | tf_op jit(solution)/shard_map/all_to_all | solution.py:87
  93.1 6.2 %gather_fusion.3 = bf16[768,896]{1,0:T(8,128)(2,1)S(1)} fusion(bf16[2304,896]{1,0:T(8,128)(2,1)} %bitcast.7, s32[1024]{0:T(1024)S(1)} %pad_clamp_fusion), kind=kCustom, calls=%fused_computation.3 | custom fusion | bytes 2755584 | tf_op jit(solution)/shard_map/jit(_take)/gather | solution.py:106
  99.3 1.3 broadcast_select_fusion.1
  103.2 7.7 %all-to-all-start.1 = ((bf16[32,1,1]{2,1,0:T(2,128)(2,1)}), bf16[32,1,1]{2,1,0:T(2,128)(2,1)S(1)}, u32[]{:S(2)}, u32[]{:S(2)}) async-start(bf16[32,1,1]{2,1,0:T(2,128)(2,1)} %copy.88), calls=%async_computation.1 | async-start | bytes 32768 | tf_op jit(solution)/shard_map/all_to_all | solution.py:89
  111.0 25.4 %all_gather.19 = bf16[3584,128]{1,0:T(8,128)(2,1)S(1)} all-gather(bf16[112,128]{1,0:T(8,128)(2,1)S(1)} %copy-done.11), channel_id=1, replica_groups=mesh['fsdp'=32,'tp'=4] {'fsdp'}, dimensions={0}, use_global_device_ids=true | all-gather | bytes 946176 | tf_op jit(solution)/shard_map/all_gather | solution.py:128
  136.4 24.3 %all_gather.21 = bf16[3584,128]{1,0:T(8,128)(2,1)S(1)} all-gather(bf16[112,128]{1,0:T(8,128)(2,1)S(1)} %copy-done.12), channel_id=1, replica_groups=mesh['fsdp'=32,'tp'=4] {'fsdp'}, dimensions={0}, use_global_device_ids=true | all-gather | bytes 946176 | tf_op jit(solution)/shard_map/all_gather | solution.py:129
  161.8 2.6 multiply_cosine_fusion
  164.4 7.9 %fusion.23 = bf16[768,512]{0,1:T(8,128)(2,1)} fusion(bf16[3584,512]{1,0:T(8,128)(2,1)} %all-gather.11.cloned.1.call-done, bf16[768,3584]{1,0:T(8,128)(2,1)} %all-gather.9.cloned.1.call-done, f32[768]{0:T(1024)S(1)} %select_reduce_fusion.2), kind=kOutput, calls=%fused_computation.48 | convolution fusion | flops 2827223040 | bytes 9964544 | tf_op jit(solution)/shard_map/dot_general | solution.py:158
  172.3 45.8 %all-gather.5.cloned.1.call-done = bf16[768,3584]{1,0:T(8,128)(2,1)} async-done(((bf16[768,896]{1,0:T(8,128)(2,1)}), bf16[768,3584]{1,0:T(8,128)(2,1)}) %all-gather.5.cloned.1.call-update) | async-done | bytes 5505040 | tf_op jit(solution)/shard_map/all_gather | solution.py:112
  218.2 3.9 fusion.8
  222.3 2.2 fusion.3
  224.5 2.0 convolution_bitcast_fusion.1
  226.5 1.5 fusion.58
  228.0 2.3 fusion.33
  230.3 36.3 %all-gather.7.cloned.1.call-done = bf16[3584,512]{1,0:T(8,128)(2,1)} async-done(((bf16[112,512]{1,0:T(8,128)(2,1)}), bf16[3584,512]{1,0:T(8,128)(2,1)}) %all-gather.7.cloned.1.call-update) | async-done | bytes 3670032 | tf_op jit(solution)/shard_map/all_gather | solution.py:127
  266.6 7.0 %fusion.74 = f32[768,512]{0,1:T(8,128)S(1)} fusion(bf16[768,3584]{1,0:T(8,128)(2,1)} %copy-done, bf16[3584,512]{1,0:T(8,128)(2,1)} %all-gather.7.cloned.1.call-done), kind=kOutput, calls=%fused_computation.142 | convolution fusion | flops 2818572288 | bytes 10747904 | tf_op jit(solution)/shard_map/dot_general | solution.py:132
  274.9 1.6 copy.121
  276.5 2.8 copy.120
  279.2 1.9 subtract_convert_fusion.1
  281.2 2.4 fusion.13
  283.6 2.3 fusion.15
  285.9 4.0 fusion.34
  290.0 3.6 fusion.9
  293.6 4.0 fusion.16
  297.6 2.0 convolution_bitcast_fusion.2
  299.6 2.0 convolution_bitcast_fusion
  303.7 6.0 %fusion.53 = f32[768,3584]{1,0:T(8,128)} fusion(bf16[3584,128]{1,0:T(8,128)(2,1)S(1)} %all_gather.19, bf16[768,64]{0,1:T(8,128)(2,1)S(1)} %get-tuple-element.39, bf16[768,64]{0,1:T(8,128)(2,1)S(1)} %get-tuple-element.38), kind=kOutput, calls=%fused_computation.82 | convolution fusion | flops 705036288 | bytes 12124160 | tf_op jit(solution)/shard_map/dot_general | solution.py:23
  309.8 5.7 %fusion.75 = f32[768,3584]{1,0:T(8,128)} fusion(bf16[768,512]{0,1:T(8,128)(2,1)S(1)} %bitcast.163, bf16[3584,512]{1,0:T(8,128)(2,1)S(1)} %copy-done.15), kind=kOutput, calls=%fused_computation.143 | convolution fusion | flops 2818572288 | bytes 15466496 | tf_op jit(solution)/shard_map/dot_general | solution.py:23
  315.5 12.6 %fusion.4 = (f32[768]{0:T(1024)S(1)}, f32[768,3584]{1,0:T(8,128)}) fusion(bf16[768,3584]{1,0:T(8,128)(2,1)S(1)} %bitcast.157, f32[768]{0:T(1024)S(1)} %add_rsqrt_fusion, f32[3584]{0:T(1024)S(1)} %convert_element_type.149, bf16[768,128]{0,1:T(8,128)(2,1)S(1)} %copy-done.10, bf16[3584,128]{1,0:T(8,128)(2,1)S(1)} %copy-done.5, f32[768,3584]{1,0:T(8,128)} %fusion.75, ...), kind=kOutput, calls=%fused_computation.10 | convolution fusion | flops 723909888 | bytes 39669760 | tf_op jit(solution)/shard_map/dot_general | solution.py:23
  328.2 8.7 %fusion.7 = bf16[768,3584]{1,0:T(8,128)(2,1)} fusion(f32[768,3584]{1,0:T(8,128)} %get-tuple-element.57, bf16[768,3584]{1,0:T(8,128)(2,1)S(1)} %bitcast.157, f32[768]{0:T(1024)S(1)} %broadcast_multiply_fusion, f32[768]{0:T(1024)S(1)} %add_rsqrt_fusion), kind=kLoop, calls=%fused_computation.13 | loop fusion | flops 16515072 | bytes 22026240 | tf_op jit(solution)/shard_map/convert_element_type | solution.py:192
  336.9 8.3 %copy.116 = bf16[768,3584]{0,1:T(8,128)(2,1)} copy(bf16[768,3584]{1,0:T(8,128)(2,1)} %fusion.7) | data formatting | bytes 11010048
  345.5 3.6 convolution_convert_fusion.3
  349.1 3.6 convolution_convert_fusion.2
  352.7 6.7 %convolution_convert_fusion.1 = bf16[3584,512]{0,1:T(8,128)(2,1)S(1)} fusion(bf16[768,512]{0,1:T(8,128)(2,1)S(1)} %bitcast.164, bf16[768,3584]{1,0:T(8,128)(2,1)} %copy-done), kind=kOutput, calls=%fused_computation.30 | convolution fusion | flops 2820407296 | bytes 9961472 | tf_op jit(solution)/shard_map/dot_general | solution.py:17
  359.5 3.4 fusion.24
  363.0 3.5 convolution_convert_fusion
  366.5 4.1 pad_maximum_fusion
  370.6 12.9 %copy.118 = bf16[3584,1280]{1,0:T(8,128)(2,1)} copy(bf16[3584,1280]{0,1:T(8,128)(2,1)} %pad_maximum_fusion) | data formatting | bytes 18350080
  383.5 18.7 %reduce-scatter.7.cloned.1.call-done = bf16[896,768]{1,0:T(8,128)(2,1)} async-done(((bf16[3584,768]{1,0:T(8,128)(2,1)}), bf16[896,768]{1,0:T(8,128)(2,1)}) %reduce-scatter.7.cloned.1.call-update) | async-done | bytes 1376272
  402.2 1.8 copy.117
  404.0 1.6 add_convert_fusion
  405.6 93.0 %reduce-scatter.9.cloned.1.call-done = bf16[112,1280]{1,0:T(8,128)(2,1)} async-done(((bf16[3584,1280]{1,0:T(8,128)(2,1)}), bf16[112,1280]{1,0:T(8,128)(2,1)}) %reduce-scatter.9.cloned.1.call-update) | async-done | bytes 286736
  498.5 1.4 fusion.73
  499.9 1.7 fusion.72
  (118 shorter events, 13.0 us)
Async XLA Ops:
  7.2 157.2 %all-gather.11.cloned.1.call-start = ((), (), s32[]{:S(2)}) async-start(), calls=%async_computation.8 | async-start | bytes 3784704 | tf_op jit(solution)/shard_map/all_gather | solution.py:130
  7.9 156.5 %all-gather.9.cloned.1.call-start = ((), (), s32[]{:S(2)}) async-start(), calls=%async_computation.7 | async-start | bytes 6881280 | tf_op jit(solution)/shard_map/all_gather | solution.py:113
  11.1 18.4 %all-to-all-start = ((bf16[32,1,1]{2,1,0:T(2,128)(2,1)}), bf16[32,1,1]{2,1,0:T(2,128)(2,1)S(1)}, u32[]{:S(2)}, u32[]{:S(2)}) async-start(bf16[32,1,1]{2,1,0:T(2,128)(2,1)} %copy.87), calls=%async_computation | async-start | bytes 32768 | tf_op jit(solution)/shard_map/all_to_all | solution.py:88
  29.5 7.6 %copy-start.14 = (s32[1,32]{1,0:T(1,128)S(1)}, s32[1,32]{1,0:T(1,128)}, u32[]{:S(2)}) copy-start(s32[1,32]{1,0:T(1,128)} %param.12) | copy-start | bytes 388
  29.5 63.6 %all-to-all-start.2 = ((bf16[32,72,896]{2,1,0:T(8,128)(2,1)}), bf16[32,72,896]{2,1,0:T(8,128)(2,1)}, u32[]{:S(2)}, u32[]{:S(2)}) async-start(bf16[32,72,896]{2,1,0:T(8,128)(2,1)} %broadcast_select_fusion), calls=%async_computation.2 | async-start | bytes 8257536 | tf_op jit(solution)/shard_map/all_to_all | solution.py:87
  37.1 181.1 %all-gather.5.cloned.1.call-start = ((), (), s32[]{:S(2)}) async-start(), calls=%async_computation.5 | async-start | bytes 6881280 | tf_op jit(solution)/shard_map/all_gather | solution.py:112
  93.1 8.2 %copy-start.16 = (s32[32]{0:T(128)S(1)}, s32[32]{0:T(128)}, u32[]{:S(2)}) copy-start(s32[32]{0:T(128)} %param.13) | copy-start | bytes 388
  93.1 17.9 %copy-start.11 = (bf16[112,128]{1,0:T(8,128)(2,1)S(1)}, bf16[112,128]{1,0:T(8,128)(2,1)}, u32[]{:S(2)}) copy-start(bf16[112,128]{1,0:T(8,128)(2,1)} %param.17) | copy-start | bytes 86020
  99.3 37.1 %copy-start.12 = (bf16[112,128]{1,0:T(8,128)(2,1)S(1)}, bf16[112,128]{1,0:T(8,128)(2,1)}, u32[]{:S(2)}) copy-start(bf16[112,128]{1,0:T(8,128)(2,1)} %param.18) | copy-start | bytes 86020
  99.3 61.4 %copy-start.13 = (bf16[3584]{0:T(1024)(128)(2,1)S(1)}, bf16[3584]{0:T(1024)(128)(2,1)}, u32[]{:S(2)}) copy-start(bf16[3584]{0:T(1024)(128)(2,1)} %param.15) | copy-start | bytes 21508
  100.7 165.9 %all-gather.7.cloned.1.call-start = ((), (), s32[]{:S(2)}) async-start(), calls=%async_computation.6 | async-start | bytes 3784704 | tf_op jit(solution)/shard_map/all_gather | solution.py:127
  103.2 57.5 %all-to-all-start.1 = ((bf16[32,1,1]{2,1,0:T(2,128)(2,1)}), bf16[32,1,1]{2,1,0:T(2,128)(2,1)S(1)}, u32[]{:S(2)}, u32[]{:S(2)}) async-start(bf16[32,1,1]{2,1,0:T(2,128)(2,1)} %copy.88), calls=%async_computation.1 | async-start | bytes 32768 | tf_op jit(solution)/shard_map/all_to_all | solution.py:89
  110.9 291.3 %reduce-scatter.7.cloned.1.call-start = ((), (), s32[]{:S(2)}) async-start(), calls=%async_computation.9 | async-start | bytes 6881280
  160.7 67.4 %copy-start.4 = (bf16[3584,128]{1,0:T(8,128)(2,1)}, bf16[3584,128]{1,0:T(8,128)(2,1)S(1)}, u32[]{:S(2)}) copy-start(bf16[3584,128]{1,0:T(8,128)(2,1)S(1)} %all_gather.21) | copy-start | bytes 2752516
  218.2 4.2 copy-start.1
  224.5 3.5 copy-start
  279.2 1.9 copy-start.7
  279.2 1.9 copy-start.8
  283.6 10.0 %copy-start.2 = (f32[768,768,4]{1,0,2:T(8,128)}, f32[768,768,4]{1,0,2:T(8,128)S(1)}, u32[]{:S(2)}) copy-start(f32[768,768,4]{1,0,2:T(8,128)S(1)} %get-tuple-element.53) | copy-start | bytes 28311556
  283.6 2.3 copy-start.17
  285.9 4.0 copy-start.18
  297.6 2.0 copy-start.9
  297.6 4.0 copy-start.6
  303.7 6.1 %copy-start.15 = (bf16[3584,512]{1,0:T(8,128)(2,1)S(1)}, bf16[3584,512]{1,0:T(8,128)(2,1)}, u32[]{:S(2)}) copy-start(bf16[3584,512]{1,0:T(8,128)(2,1)} %all-gather.7.cloned.1.call-done) | copy-start | bytes 11010052
  303.7 11.8 %slice-start = ((s8[5505024]{0:T(1024)(128)(4,1)}), s8[4194304]{0:T(1024)(128)(4,1)S(1)}, s32[]{:S(2)}) async-start(s8[5505024]{0:T(1024)(128)(4,1)} %bitcast.156), calls=%async_computation.11 | async-start | bytes 8388608
  309.8 5.7 %slice-start.1 = ((s8[5505024]{0:T(1024)(128)(4,1)}), s8[1310720]{0:T(1024)(128)(4,1)S(1)}, s32[]{:S(2)}) async-start(s8[5505024]{0:T(1024)(128)(4,1)} %bitcast.156), calls=%async_computation.12 | async-start | bytes 2621440
  309.8 5.7 %copy-start.5 = (bf16[3584,128]{1,0:T(8,128)(2,1)S(1)}, bf16[3584,128]{1,0:T(8,128)(2,1)}, u32[]{:S(2)}) copy-start(bf16[3584,128]{1,0:T(8,128)(2,1)} %copy-done.4) | copy-start | bytes 2752516
  309.8 5.7 %copy-start.10 = (bf16[768,128]{0,1:T(8,128)(2,1)S(1)}, bf16[768,128]{0,1:T(8,128)(2,1)}, u32[]{:S(2)}) copy-start(bf16[768,128]{0,1:T(8,128)(2,1)} %fusion.34) | copy-start | bytes 589828
  345.2 153.3 %reduce-scatter.9.cloned.1.call-start = ((), (), s32[]{:S(2)}) async-start(), calls=%async_computation.10 | async-start | bytes 9461760
  345.5 14.0 %slice-start.2 = ((s8[9437184]{0:T(1024)(128)(4,1)}), s8[4194304]{0:T(1024)(128)(4,1)S(1)}, s32[]{:S(2)}) async-start(s8[9437184]{0:T(1024)(128)(4,1)} %bitcast.158), calls=%async_computation.13 | async-start | bytes 8388608
  349.1 10.4 %slice-start.3 = ((s8[9437184]{0:T(1024)(128)(4,1)}), s8[4194304]{0:T(1024)(128)(4,1)S(1)}, s32[]{:S(2)}) async-start(s8[9437184]{0:T(1024)(128)(4,1)} %bitcast.158), calls=%async_computation.14 | async-start | bytes 8388608
  352.7 6.8 %slice-start.4 = ((s8[9437184]{0:T(1024)(128)(4,1)}), s8[1048576]{0:T(1024)(128)(4,1)S(1)}, s32[]{:S(2)}) async-start(s8[9437184]{0:T(1024)(128)(4,1)} %bitcast.158), calls=%async_computation.15 | async-start | bytes 2097152
  352.7 6.8 %copy-start.19 = (bf16[768,128,1]{1,0,2:T(8,128)(2,1)S(1)}, bf16[768,128,1]{1,0,2:T(8,128)(2,1)}, u32[]{:S(2)}) copy-start(bf16[768,128,1]{1,0,2:T(8,128)(2,1)} %fusion.33) | copy-start | bytes 589828
  352.7 10.2 %slice-start.5 = ((s8[5505024]{0:T(1024)(128)(4,1)}), s8[4194304]{0:T(1024)(128)(4,1)S(1)}, s32[]{:S(2)}) async-start(s8[5505024]{0:T(1024)(128)(4,1)} %bitcast.166), calls=%async_computation.16 | async-start | bytes 8388608
  359.5 3.5 slice-start.6
  383.5 20.5 %copy-start.3 = (bf16[768,896]{1,0:T(8,128)(2,1)S(1)}, bf16[768,896]{1,0:T(8,128)(2,1)}, u32[]{:S(2)}) copy-start(bf16[768,896]{1,0:T(8,128)(2,1)} %param.14) | copy-start | bytes 4128772
Sparse Core Ops, SparseCore 0:
  10.3 81.4 all-gather.10
  93.5 62.5 all-gather.8
  158.4 59.7 all-gather.4
  220.3 46.2 all-gather.6
  345.4 56.7 reduce-scatter.6
  405.8 92.6 reduce-scatter.8
where the time goes:
time: 518 us; the launch traced here: 509 us
  waiting for transfers between devices  250 us (48%)
  matrix products  78.4 us (15%)
  blocking collectives  49.7 us (10%)
  local copies, waits for them, and re-layouts  46.9 us (9%)
  other arithmetic  44.1 us (9%)
  starting transfers between devices  24.3 us (5%)
  between operations  14.9 us (3%)
    unnamed x8, waiting for transfers between devices  114 us
    all_to_all x1, waiting for transfers between devices, per_device(): lax.all_to_all(send_rows, 'fsdp', split_axis=0, concat_axis=0, tiled=True)  54.6 us
    all_gather x1, waiting for transfers between devices, per_device(): lax.all_gather(learner_rows, 'tp', axis=1, tiled=True)  45.8 us
    all_gather x1, waiting for transfers between devices, per_device(): lax.all_gather(w_q, 'fsdp', axis=0, tiled=True)  36.3 us
    unnamed x59, local copies, waits for them, and re-layouts  27.8 us
    all_gather x1, blocking collectives, per_device(): lax.all_gather(w_k, 'fsdp', axis=0, tiled=True)  25.4 us
    dot_general x3, matrix products, times_trans(): lax.dot_general(left, right, (((1,), (1,)), ((), ())), preferred_element_...  24.4 us
    all_gather x1, blocking collectives, per_device(): lax.all_gather(w_v, 'fsdp', axis=0, tiled=True)  24.3 us
  transfers between devices with their start and end apart: 9, of which 5 were waited for; matrix products, arithmetic and copies ran while one was open for 17% of the time, Pallas kernels for 0%

commit v1 on v0

v1 whole, which is shorter than its diff:
```python
import jax
import jax.numpy as jnp
import numpy as np
from jax import lax
from jax.experimental import pallas as pl
from jax.experimental.pallas import tpu as pltpu
from jax.sharding import PartitionSpec as P

HD = 128
GSIZE = 16
ROPE_BASE = 1000000.0
NORM_EPSILON = 1e-06
MESH = pl.DeviceIdType.MESH
BF = jnp.bfloat16
F32 = jnp.float32
HBM = pl.BlockSpec(memory_space=pl.ANY)
VMEM = pl.BlockSpec(memory_space=pltpu.VMEM)
SMEM = pl.BlockSpec(memory_space=pltpu.SMEM)
DMA = pltpu.SemaphoreType.DMA
LIMIT = 56 * 2**20

N_F = 32
N_Z = 4
SEQ = 32
MAXLEN = 72
TOK = 768
HALF = TOK // 2
FB = 896
D = 3584
QC = 512
KC = 128
TB = 128

CHIPS = [(0, 1), (1, 0), (0, 3), (3, 0), (1, 1), (3, 3), (1, 3), (3, 1),
         (0, 2), (2, 0), (1, 2), (2, 1), (3, 2), (2, 3), (2, 2)]
OFFSETS = [(0, 0, 1)] + [(a, b, c) for c in range(2) for a, b in CHIPS]


def nt(a, b):
    return lax.dot_general(a, b, (((1,), (1,)), ((), ())), preferred_element_type=F32)


def tn(a, b):
    return lax.dot_general(a, b, (((0,), (0,)), ((), ())), preferred_element_type=F32)


def nn(a, b):
    return lax.dot_general(a, b, (((1,), (0,)), ((), ())), preferred_element_type=F32)


def iota(shape, dim):
    return lax.broadcasted_iota(jnp.int32, shape, dim)


def stage_kernel(dest_s, dest_r, clus_r, clus_c, roll, send, meta, sem):
    def start(s, c):
        t = dest_s[s] // SEQ
        pltpu.make_async_copy(roll.at[s], send.at[t], sem.at[s]).start()
        return c

    lax.fori_loop(0, SEQ, start, 0)
    same = (clus_c[...] == clus_r[...]) & (iota((SEQ, SEQ), 0) // GSIZE == iota((SEQ, SEQ), 1) // GSIZE)
    group = iota((SEQ, SEQ), 0) // GSIZE == iota((SEQ, SEQ), 1) // GSIZE
    same = jnp.where(same, 1.0 / GSIZE, 0.0)
    share_c = jnp.sum(same, axis=1, keepdims=True)
    share_r = jnp.sum(same, axis=0, keepdims=True)
    mean_r = jnp.sum(jnp.where(group, share_c, 0.0), axis=0, keepdims=True) * (1.0 / GSIZE)
    adv_r = (share_r - mean_r).astype(BF).astype(F32)
    rows = iota((SEQ * 8, SEQ), 0)
    dest_v = dest_r[...]
    hit = dest_v // SEQ == rows // 8
    what = jnp.where(rows % 8 < 4, (dest_v % SEQ).astype(F32), adv_r)
    meta[...] = jnp.broadcast_to(jnp.sum(jnp.where(hit, what, 0.0), axis=1, keepdims=True), (SEQ * 8, 128))

    def wait(s, c):
        t = dest_s[s] // SEQ
        pltpu.make_async_copy(roll.at[s], send.at[t], sem.at[s]).wait()
        return c

    lax.fori_loop(0, SEQ, wait, 0)


def ring_copy(src, dst, blk, half, to, ss, rs, i):
    sl = pl.ds(half * HALF, HALF)
    return pltpu.make_async_remote_copy(
        src_ref=src.at[sl], dst_ref=dst.at[blk, sl], send_sem=ss.at[i], recv_sem=rs.at[i],
        device_id={"tp": to}, device_id_type=MESH)


def ring_start(own, dst, z, ss, rs):
    right, left = lax.rem(z + 1, N_Z), lax.rem(z + 3, N_Z)
    c = [ring_copy(own, dst, z, 0, right, ss, rs, 0), ring_copy(own, dst, z, 1, left, ss, rs, 1),
         ring_copy(own, dst, z, 1, right, ss, rs, 2), ring_copy(own, dst, z, 0, left, ss, rs, 3)]
    for x in c:
        x.start()
    return c


def ring_end(own, dst, z, ss, rs, c):
    right, left, far = lax.rem(z + 1, N_Z), lax.rem(z + 3, N_Z), lax.rem(z + 2, N_Z)
    ring_copy(own, dst, left, 0, right, ss, rs, 0).wait_recv()
    f0 = ring_copy(dst.at[left], dst, left, 0, right, ss, rs, 4)
    f0.start()
    ring_copy(own, dst, right, 1, left, ss, rs, 1).wait_recv()
    f1 = ring_copy(dst.at[right], dst, right, 1, left, ss, rs, 5)
    f1.start()
    ring_copy(own, dst, left, 1, right, ss, rs, 2).wait_recv()
    ring_copy(own, dst, right, 0, left, ss, rs, 3).wait_recv()
    ring_copy(own, dst, far, 0, right, ss, rs, 4).wait_recv()
    ring_copy(own, dst, far, 1, left, ss, rs, 5).wait_recv()
    for x in c + [f0, f1]:
        x.wait_send()


def hand_kernel(send, meta, cot, out, meta_out, cot_full, lsem, ss, rs, ms, mr, zs, zr):
    me = lax.axis_index("fsdp")
    z = lax.axis_index("tp")
    y, x, c = me // 8, (me // 2) % 4, me % 2

    def peer(o, s):
        return lax.rem(y + s * o[0] + 4, 4) * 8 + lax.rem(x + s * o[1] + 4, 4) * 2 + lax.rem(c + s * o[2] + 2, 2)

    barrier = pltpu.get_barrier_semaphore()
    for o in OFFSETS:
        pl.semaphore_signal(barrier, inc=1, device_id={"fsdp": peer(o, 1)}, device_id_type=MESH)
    for d in (1, 3):
        pl.semaphore_signal(barrier, inc=1, device_id={"tp": lax.rem(z + d, N_Z)}, device_id_type=MESH)
    pl.semaphore_wait(barrier, len(OFFSETS) + 2)
    mine = [pltpu.make_async_copy(send.at[me], out.at[me], lsem.at[0]),
            pltpu.make_async_copy(meta.at[pl.ds(8 * me, 8)], meta_out.at[pl.ds(8 * me, 8)], lsem.at[1]),
            pltpu.make_async_copy(cot, cot_full.at[z], lsem.at[2])]
    ring = ring_start(cot, cot_full, z, zs, zr)

    def slab(i, frm, to, who):
        return pltpu.make_async_remote_copy(
            src_ref=send.at[frm], dst_ref=out.at[to], send_sem=ss.at[i], recv_sem=rs.at[i],
            device_id={"fsdp": who}, device_id_type=MESH)

    def note(i, frm, to, who):
        return pltpu.make_async_remote_copy(
            src_ref=meta.at[pl.ds(8 * frm, 8)], dst_ref=meta_out.at[pl.ds(8 * to, 8)],
            send_sem=ms.at[i], recv_sem=mr.at[i], device_id={"fsdp": who}, device_id_type=MESH)

    for i, o in enumerate(OFFSETS):
        t = peer(o, 1)
        slab(i, t, me, t).start()
        note(i, t, me, t).start()
    for m in mine:
        m.start()
    ring_end(cot, cot_full, z, zs, zr, ring)
    for i, o in enumerate(OFFSETS):
        t, f = peer(o, 1), peer(o, -1)
        slab(i, t, f, t).wait_recv()
        note(i, t, f, t).wait_recv()
        slab(i, t, me, t).wait_send()
        note(i, t, me, t).wait_send()
    for m in mine:
        m.wait()


def pack_kernel(rows, meta, len_c, gain, table, packed, scaled, squares, rope, pos_b, adv_b, keys):
    lane = iota((SEQ, 128), 1)
    sub = iota((SEQ, 128), 0)
    lens = len_c[...].astype(F32)
    ends = jnp.sum(jnp.where(sub <= lane, lens, 0.0), axis=0, keepdims=True)
    starts = jnp.sum(jnp.where(sub < lane, lens, 0.0), axis=0, keepdims=True)
    place = meta[pl.ds(0, SEQ, 8), :]
    share = meta[pl.ds(4, SEQ, 8), :]
    one = iota((1, 128), 1)
    place_r = jnp.where(one < SEQ, jnp.sum(jnp.where(sub == lane, place, 0.0), axis=0, keepdims=True), -1.0)
    share_r = jnp.sum(jnp.where(sub == lane, share, 0.0), axis=0, keepdims=True)
    column = iota((SEQ, SEQ * MAXLEN), 1)
    source = iota((SEQ, SEQ * MAXLEN), 0)
    here = (column >= source * MAXLEN) & (column < (source + 1) * MAXLEN)
    key = place[:, :1] * 128.0 + (column - source * MAXLEN).astype(F32)
    keys[...] = jnp.sum(jnp.where(here, key, 0.0), axis=0, keepdims=True)

    def block(b, c):
        at = pl.ds(pl.multiple_of(b * TB, TB), TB)
        i = (iota((TB, 128), 0) + b * TB).astype(F32)
        lane_f = iota((TB, 128), 1).astype(F32)
        hit = (i >= starts) & (i < ends)
        seg = jnp.sum(jnp.where(hit, lane_f, 0.0), axis=1, keepdims=True)
        start = jnp.sum(jnp.where(hit, starts, 0.0), axis=1, keepdims=True)
        pos = i - start
        pos_b[at, :] = pos
        adv_b[at, :] = jnp.broadcast_to(
            jnp.sum(jnp.where(place_r == seg, share_r, 0.0), axis=1, keepdims=True), (TB, 128))
        rope[at, :] = lax.dot_general(
            jnp.where(pos == lane_f, 1.0, 0.0), table[...], (((1,), (0,)), ((), ())),
            precision=lax.Precision.HIGHEST, preferred_element_type=F32)
        pick = jnp.where(seg * 128.0 + pos[:, :1] == keys[...], 1.0, 0.0).astype(BF)
        took = nn(pick, rows[...])
        packed[at, :] = took.astype(BF)
        scaled[at, :] = (took * gain[...].astype(F32)).astype(BF)
        square = jnp.sum(took * took, axis=1, keepdims=True)
        squares[:, at] = jnp.transpose(jnp.broadcast_to(square, (TB, 128)))[:8, :]
        return c

    lax.fori_loop(0, TOK // TB, block, 0)


def gather_kernel(own, sq, full, sq_full, lsem, zs, zr, qs, qr):
    z = lax.axis_index("tp")
    barrier = pltpu.get_barrier_semaphore()
    for d in (1, 2, 3):
        pl.semaphore_signal(barrier, inc=1, device_id={"tp": lax.rem(z + d, N_Z)}, device_id_type=MESH)
    pl.semaphore_wait(barrier, 3)
    mine = [pltpu.make_async_copy(own, full.at[z], lsem.at[0]), pltpu.make_async_copy(sq, sq_full.at[z], lsem.at[1])]
    ring = ring_start(own, full, z, zs, zr)

    def note(d, blk):
        return pltpu.make_async_remote_copy(
            src_ref=sq, dst_ref=sq_full.at[blk], send_sem=qs.at[d], recv_sem=qr.at[d],
            device_id={"tp": lax.rem(z + d, N_Z)}, device_id_type=MESH)

    for d in (1, 2, 3):
        note(d, z).start()
    for m in mine:
        m.start()
    ring_end(own, full, z, zs, zr, ring)
    for d in (1, 2, 3):
        note(d, lax.rem(z + N_Z - d, N_Z)).wait_recv()
        note(d, z).wait_send()
    for m in mine:
        m.wait()


def unstack(v):
    return jnp.concatenate([v[h * TB:(h + 1) * TB] for h in range(4)], axis=1)


def stack(v):
    return jnp.concatenate([v[:, h * HD:(h + 1) * HD] for h in range(4)], axis=0)


def turn(v, cos, sin):
    return v * cos + jnp.concatenate([v[:, HD // 2:], v[:, :HD // 2]], axis=1) * sin


def turn_back(v, cos, sin):
    return v * cos - jnp.concatenate([v[:, HD // 2:], v[:, :HD // 2]], axis=1) * sin


def block_kernel(xf, cf, wf, sq, rope, pos_b, adv_b, grads, outs, inv_b, dots,
                 xv, cv, wv, sem, lin, ga, qrot, kbuf, vbuf, gab, dk, dv, mq):
    copies = []
    for b in range(N_Z):
        copies.append([pltpu.make_async_copy(xf.at[b], xv.at[b], sem.at[b, 0]),
                       pltpu.make_async_copy(cf.at[b], cv.at[b], sem.at[b, 1]),
                       pltpu.make_async_copy(wf.at[b], wv.at[b], sem.at[b, 2])])
        for k in copies[-1]:
            k.start()
    total = sq[0] + sq[1] + sq[2] + sq[3]
    inv_t = lax.rsqrt(total * (1.0 / D) + NORM_EPSILON)
    for b in range(TOK // TB):
        inv_b[b * TB:(b + 1) * TB, :] = jnp.transpose(jnp.broadcast_to(inv_t[:1, b * TB:(b + 1) * TB], (128, TB)))
    kbuf[...] = jnp.zeros_like(kbuf)
    vbuf[...] = jnp.zeros_like(vbuf)
    dk[...] = jnp.zeros_like(dk)
    dv[...] = jnp.zeros_like(dv)
    lin[...] = jnp.zeros_like(lin)
    ga[...] = jnp.zeros_like(ga)
    for b in range(N_Z):
        for k in copies[b]:
            k.wait()
    def project(b, c):
        for n in range(3):
            lin[:, n * 256:(n + 1) * 256] += nn(xv[b], wv[b, :, n * 256:(n + 1) * 256])
        for n in range(2):
            ga[:, n * 256:(n + 1) * 256] += nn(cv[b], wv[b, :, 768 + n * 256:768 + (n + 1) * 256])
        return c

    lax.fori_loop(0, N_Z, project, 0)

    def ready(b, c):
        at = pl.ds(pl.multiple_of(b * TB, TB), TB)
        up = pl.ds(pl.multiple_of(b * TB + TB, TB), TB)
        inv = inv_b[at, :]
        cos, sin = rope[at, :HD], rope[at, HD:]
        for h in range(4):
            qrot[at, h * HD:(h + 1) * HD] = turn(lin[at, h * HD:(h + 1) * HD] * inv, cos, sin).astype(BF)
            gab[at, h * HD:(h + 1) * HD] = (ga[at, h * HD:(h + 1) * HD] * adv_b[at, :]).astype(BF)
        kbuf[up, :] = turn(lin[at, QC:QC + KC] * inv, cos, sin).astype(BF)
        vbuf[up, :] = (lin[at, QC + KC:] * inv).astype(BF)
        return c

    lax.fori_loop(0, TOK // TB, ready, 0)
    scale = HD ** (-0.5)

    def attend(b, c):
        at = pl.ds(pl.multiple_of(b * TB, TB), TB)
        win = pl.ds(pl.multiple_of(b * TB, TB), 2 * TB)
        q = stack(qrot[at, :])
        g = stack(gab[at, :])
        k, v = kbuf[win, :], vbuf[win, :]
        back = iota((TB, 2 * TB), 0) + TB - iota((TB, 2 * TB), 1)
        ok = (back >= 0) & (back.astype(F32) <= pos_b[at, :1])
        ok = jnp.concatenate([ok] * 4, axis=0)
        s = jnp.where(ok, nt(q, k) * scale, -1e30)
        e = jnp.where(ok, jnp.exp(s - jnp.max(s, axis=1, keepdims=True)), 0.0)
        p = e / jnp.sum(e, axis=1, keepdims=True)
        pb = p.astype(BF)
        o = unstack(nn(pb, v))
        dp = nt(g, v)
        ds = (p * (dp - jnp.sum(p * dp, axis=1, keepdims=True)) * scale).astype(BF)
        dq = nn(ds, k)
        dk[win, :] += tn(ds, q)
        dv[win, :] += tn(pb, g)
        prod = dq * q.astype(F32)
        mq[at, :] = prod[:TB] + prod[TB:2 * TB] + prod[2 * TB:3 * TB] + prod[3 * TB:]
        dq = unstack(dq)
        inv = inv_b[at, :]
        cos, sin = rope[at, :HD], rope[at, HD:]
        for h in range(4):
            col = slice(h * HD, (h + 1) * HD)
            grads[at, col] = (turn_back(dq[:, col], cos, sin) * inv).astype(BF)
            outs[at, col] = (o[:, col] * adv_b[at, :]).astype(BF)
        return c

    lax.fori_loop(0, TOK // TB, attend, 0)

    def finish(b, c):
        at = pl.ds(pl.multiple_of(b * TB, TB), TB)
        up = pl.ds(pl.multiple_of(b * TB + TB, TB), TB)
        inv = inv_b[at, :]
        cos, sin = rope[at, :HD], rope[at, HD:]
        gk, gv = dk[up, :], dv[up, :]
        grads[at, QC:QC + KC] = (turn_back(gk, cos, sin) * inv).astype(BF)
        grads[at, QC + KC:] = (gv * inv).astype(BF)
        m = mq[at, :] + gk * kbuf[up, :].astype(F32) + gv * vbuf[up, :].astype(F32)
        m = jnp.sum(m, axis=1, keepdims=True) * inv
        dots[:, at] = jnp.transpose(m)[:8, :]
        return c

    lax.fori_loop(0, TOK // TB, finish, 0)


def input_kernel(grads, wf, dots, packed, lpg, gain, inv_b, adv_b, result,
                 wv, dots_all, sbuf, rbuf, own, wsem, zs, zr, ds_, dr):
    z = lax.axis_index("tp")
    right, left, far = lax.rem(z + 1, N_Z), lax.rem(z + 3, N_Z), lax.rem(z + 2, N_Z)
    order = [far, right, left, z]
    loads = [pltpu.make_async_copy(wf.at[t, :, pl.ds(0, QC + 2 * KC)], wv.at[i], wsem.at[i]) for i, t in enumerate(order)]
    for k in loads:
        k.start()
    barrier = pltpu.get_barrier_semaphore()
    for d in (1, 2, 3):
        pl.semaphore_signal(barrier, inc=1, device_id={"tp": lax.rem(z + d, N_Z)}, device_id_type=MESH)
    pl.semaphore_wait(barrier, 3)

    def note(d, blk):
        return pltpu.make_async_remote_copy(
            src_ref=dots, dst_ref=dots_all.at[d - 1], send_sem=ds_.at[d], recv_sem=dr.at[d],
            device_id={"tp": lax.rem(z + d, N_Z)}, device_id_type=MESH)

    for d in (1, 2, 3):
        note(d, z).start()

    def ship(i, to):
        return pltpu.make_async_remote_copy(
            src_ref=sbuf.at[i], dst_ref=rbuf.at[i], send_sem=zs.at[i], recv_sem=zr.at[i],
            device_id={"tp": to}, device_id_type=MESH)

    def share(i, h):
        return nt(grads[h * HALF:(h + 1) * HALF, :], wv[i])

    loads[0].wait()
    sbuf[0] = share(0, 0).astype(BF)
    ship(0, right).start()
    sbuf[1] = share(0, 1).astype(BF)
    ship(1, left).start()
    loads[1].wait()
    sbuf[2] = share(1, 1).astype(BF)
    ship(2, right).start()
    loads[2].wait()
    sbuf[3] = share(2, 0).astype(BF)
    ship(3, left).start()
    a = share(1, 0)
    ship(0, right).wait_recv()
    sbuf[4] = (a + rbuf[0].astype(F32)).astype(BF)
    ship(4, right).start()
    a = share(2, 1)
    ship(1, left).wait_recv()
    sbuf[5] = (a + rbuf[1].astype(F32)).astype(BF)
    ship(5, left).start()
    loads[3].wait()
    own[:HALF] = share(3, 0)
    own[HALF:] = share(3, 1)
    for d in (1, 2, 3):
        note(d, z).wait_recv()
        note(d, z).wait_send()
    m = (dots[...] + dots_all[0] + dots_all[1] + dots_all[2]) * (1.0 / D)
    ship(2, right).wait_recv()
    ship(3, left).wait_recv()
    ship(4, right).wait_recv()
    ship(5, left).wait_recv()
    for b in range(TOK // TB):
        h, r = divmod(b * TB, HALF)
        at = slice(b * TB, (b + 1) * TB)
        hs = slice(r, r + TB)
        one, two = (4, 3) if h == 0 else (2, 5)
        s = own[at, :] + rbuf[one, hs, :].astype(F32) + rbuf[two, hs, :].astype(F32)
        mc = jnp.transpose(jnp.broadcast_to(m[:1, at], (128, TB)))[:, :1]
        inv = inv_b[at, :1]
        result[at, :] = (adv_b[at, :1] * lpg[at, :].astype(F32) + s * gain[...].astype(F32)
                         - packed[at, :].astype(F32) * (inv * mc)).astype(BF)
    for i in range(6):
        ship(i, right if i % 2 == 0 else left).wait_send()


def sds(shape, dtype=BF):
    return jax.ShapeDtypeStruct(shape, dtype)


def params(**kw):
    return pltpu.CompilerParams(vmem_limit_bytes=LIMIT, has_side_effects=True, **kw)


def rope_table():
    i = np.arange(HD // 2, dtype=np.float32)
    frequency = np.float32(ROPE_BASE) ** (-(np.float32(2.0) * i) / np.float32(HD))
    angle = np.arange(128, dtype=np.float32)[:, None] * frequency[None, :]
    c, s = np.cos(angle), np.sin(angle)
    return np.concatenate([c, c, -s, s], axis=1).astype(np.float32)


def per_device(roll_rows, dest, lengths, clusters, log_prob_grad, gain, w_q, w_k, w_v, w_o_t):
    z = lax.axis_index("tp")
    weights = lax.all_gather(jnp.concatenate([w_q, w_k, w_v, w_o_t], axis=1), "fsdp", axis=0, tiled=True)
    weights = weights.reshape(N_Z, FB, QC * 2 + KC * 2)
    gain_own = lax.dynamic_slice(gain, (z * FB,), (FB,)).reshape(1, FB)
    send, meta = pl.pallas_call(
        stage_kernel, out_shape=(sds((SEQ, MAXLEN, FB)), sds((SEQ * 8, 128), F32)),
        in_specs=[SMEM, VMEM, VMEM, VMEM, HBM], out_specs=(HBM, VMEM),
        scratch_shapes=[DMA((SEQ,))], compiler_params=params(),
    )(dest, dest.reshape(1, SEQ), clusters.reshape(1, SEQ), clusters.reshape(SEQ, 1), roll_rows)
    n_o = len(OFFSETS)
    arrived, meta_in, cot = pl.pallas_call(
        hand_kernel, out_shape=(sds((SEQ, MAXLEN, FB)), sds((SEQ * 8, 128), F32), sds((N_Z, TOK, FB))),
        in_specs=[HBM, HBM, HBM], out_specs=(HBM, HBM, HBM),
        scratch_shapes=[DMA((3,)), DMA((n_o,)), DMA((n_o,)), DMA((n_o,)), DMA((n_o,)), DMA((6,)), DMA((6,))],
        compiler_params=params(collective_id=0),
    )(send, meta, log_prob_grad)
    packed, scaled, squares, rope, pos_b, adv_b = pl.pallas_call(
        pack_kernel,
        out_shape=(sds((TOK, FB)), sds((TOK, FB)), sds((8, TOK), F32), sds((TOK, 2 * HD), F32),
                   sds((TOK, 128), F32), sds((TOK, 128), F32)),
        in_specs=[VMEM] * 5, out_specs=(VMEM,) * 6,
        scratch_shapes=[pltpu.VMEM((1, SEQ * MAXLEN), F32)], compiler_params=params(),
    )(arrived.reshape(SEQ * MAXLEN, FB), meta_in, lengths.reshape(SEQ, 1), gain_own, jnp.asarray(rope_table()))
    rows, sq = pl.pallas_call(
        gather_kernel, out_shape=(sds((N_Z, TOK, FB)), sds((N_Z, 8, TOK), F32)),
        in_specs=[HBM, HBM], out_specs=(HBM, HBM),
        scratch_shapes=[DMA((2,)), DMA((6,)), DMA((6,)), DMA((4,)), DMA((4,))],
        compiler_params=params(collective_id=1),
    )(scaled, squares)
    grads, outs, inv_b, dots = pl.pallas_call(
        block_kernel,
        out_shape=(sds((TOK, QC + 2 * KC)), sds((TOK, QC)), sds((TOK, 128), F32), sds((8, TOK), F32)),
        in_specs=[HBM, HBM, HBM] + [VMEM] * 4, out_specs=(VMEM,) * 4,
        scratch_shapes=[
            pltpu.VMEM((N_Z, TOK, FB), BF), pltpu.VMEM((N_Z, TOK, FB), BF),
            pltpu.VMEM((N_Z, FB, 2 * QC + 2 * KC), BF), DMA((N_Z, 3)),
            pltpu.VMEM((TOK, QC + 2 * KC), F32), pltpu.VMEM((TOK, QC), F32),
            pltpu.VMEM((TOK, QC), BF), pltpu.VMEM((TOK + TB, HD), BF), pltpu.VMEM((TOK + TB, HD), BF),
            pltpu.VMEM((TOK, QC), BF), pltpu.VMEM((TOK + TB, HD), F32), pltpu.VMEM((TOK + TB, HD), F32),
            pltpu.VMEM((TOK, HD), F32)],
        compiler_params=params(),
    )(rows, cot, weights, sq, rope, pos_b, adv_b)
    def terms(left, right):
        t = lax.dot_general(left, right, (((1,), (0,)), ((), ())), preferred_element_type=F32)
        return t.astype(BF).reshape(D, right.shape[1])

    total = lax.psum_scatter(
        jnp.concatenate([terms(rows, grads), terms(cot, outs)], axis=1), "fsdp", scatter_dimension=0, tiled=True)
    input_grad = pl.pallas_call(
        input_kernel, out_shape=sds((TOK, FB)),
        in_specs=[VMEM, HBM] + [VMEM] * 6, out_specs=VMEM,
        scratch_shapes=[
            pltpu.VMEM((N_Z, FB, QC + 2 * KC), BF), pltpu.VMEM((3, 8, TOK), F32),
            pltpu.VMEM((6, HALF, FB), BF), pltpu.VMEM((6, HALF, FB), BF), pltpu.VMEM((TOK, FB), F32),
            DMA((N_Z,)), DMA((6,)), DMA((6,)), DMA((4,)), DMA((4,))],
        compiler_params=params(collective_id=2),
    )(grads, weights, dots, packed, log_prob_grad, gain_own, inv_b, adv_b)
    a, b, c = QC, QC + KC, QC + 2 * KC
    return (input_grad, total[:, :a], total[:, a:b], total[:, b:c], total[:, c:])


def solution(mesh):
    in_specs = (
        P("fsdp", None, "tp"), P("fsdp"), P("fsdp", None), P("fsdp"), P("fsdp", "tp"), P(),
        P("fsdp", "tp"), P("fsdp", "tp"), P("fsdp", "tp"), P("fsdp", "tp"),
    )
    out_specs = (P("fsdp", "tp"),) * 5
    return jax.shard_map(per_device, mesh=mesh, in_specs=in_specs, out_specs=out_specs, check_vma=False)
```

time: 518 us -> 411 us (0.79); the launches traced: 509 us -> 410 us
  Pallas kernels: 0 us -> 330 us
  waiting for transfers between devices: 250 us -> 40.2 us
  matrix products: 78.4 us -> 9.4 us
  blocking collectives: 49.7 us -> 0 us
  other arithmetic: 44.1 us -> 5.7 us
  local copies, waits for them, and re-layouts: 46.9 us -> 9.61 us
  starting transfers between devices: 24.3 us -> 0.08 us
    pallas_call x0 -> x6, Pallas kernels: none -> 330 us  [the longest x1 128 us: per_device(): pl.pallas_call(stage_kernel, out_shape=(sds((SEQ, MAXLEN, FB)), sds((SEQ...]
    unnamed x8 -> x2, waiting for transfers between devices: 114 us -> 0.03 us
    all_gather x4 -> x1, waiting for transfers between devices: 82.1 us -> 0.02 us  [per_device(): lax.all_gather(jnp.concatenate([w_q, w_k, w_v, w_o_t], axis=1), 'fsdp', a...]
    dot_general x17 -> x2, matrix products: 78.4 us -> 9.4 us  [terms(): lax.dot_general(left, right, (((1,), (0,)), ((), ())), preferred_element_...]
    all_to_all x3 -> x0, waiting for transfers between devices: 54.6 us -> none  [the longest x1 54.6 us: per_device(): lax.all_to_all(send_rows, 'fsdp', split_axis=0, concat_axis=0, tiled=True)]
    all_gather x2 -> x0, blocking collectives: 49.7 us -> none  [the longest x1 25.4 us: per_device(): lax.all_gather(w_k, 'fsdp', axis=0, tiled=True)]
    reduce_scatter x0 -> x1, waiting for transfers between devices: none -> 40.1 us  [per_device(): lax.psum_scatter(jnp.concatenate([terms(rows, grads), terms(cot, outs)],...]
    unnamed x59 -> x9, local copies, waits for them, and re-layouts: 27.8 us -> 2.54 us
  transfers between devices with their start and end apart: 9 -> 2, of which waited for: 5 -> 1; matrix products, arithmetic and copies ran while one was open for 17% -> 1% of each run, Pallas kernels for 0% -> 74%
where the time goes in v1:
time: 411 us; the launch traced here: 410 us
  Pallas kernels  330 us (80%)
  waiting for transfers between devices  40.2 us (10%)
  between operations  14.2 us (3%)
  local copies, waits for them, and re-layouts  9.61 us (2%)
  matrix products  9.4 us (2%)
  other arithmetic  5.7 us (1%)
    pallas_call x1, Pallas kernels, per_device(): pl.pallas_call(stage_kernel, out_shape=(sds((SEQ, MAXLEN, FB)), sds((SEQ...  128 us
    pallas_call x1, Pallas kernels, per_device(): pl.pallas_call(hand_kernel, out_shape=(sds((SEQ, MAXLEN, FB)), sds((SEQ *...  59.8 us
    pallas_call x1, Pallas kernels, per_device(): pl.pallas_call(input_kernel, out_shape=sds((TOK, FB)), in_specs=[VMEM, HB...  54 us
    pallas_call x1, Pallas kernels, per_device(): pl.pallas_call(gather_kernel, out_shape=(sds((N_Z, TOK, FB)), sds((N_Z, 8...  51.6 us
    reduce_scatter x1, waiting for transfers between devices, per_device(): lax.psum_scatter(jnp.concatenate([terms(rows, grads), terms(cot, outs)],...  40.1 us
    pallas_call x1, Pallas kernels, per_device(): pl.pallas_call(block_kernel, out_shape=(sds((TOK, QC + 2 * KC)), sds((TOK...  26.5 us
    pallas_call x1, Pallas kernels, per_device(): pl.pallas_call(pack_kernel, out_shape=(sds((TOK, FB)), sds((TOK, FB)), sd...  10.7 us
    dot_general x2, matrix products, terms(): lax.dot_general(left, right, (((1,), (0,)), ((), ())), preferred_element_...  9.4 us
  transfers between devices with their start and end apart: 2, of which 1 were waited for; matrix products, arithmetic and copies ran while one was open for 1% of the time, Pallas kernels for 74%

profile of v1, /device:TPU:1, one launch (start us, length us, event | category | flops | bytes accessed | tf_op | source)
XLA Modules:
  0.0 409.6 jit_solution(831475450538908820)
XLA Ops:
  7.2 0.0 all-gather.2.cloned.1.call-start
  7.2 1.7 pad_maximum_fusion.1
  8.9 0.0 all-gather.2.cloned.1.call-update
  9.0 0.0 reduce-scatter.2.cloned.1.call-start
  9.0 1.3 copy.16.clus_c
  10.4 1.3 copy.17.len_c
  11.7 0.8 dynamic_slice.3
  12.5 0.6 reshape.42.gain
  13.1 127.9 %shard_map.146 = (bf16[32,72,896]{2,1,0:T(8,128)(2,1)}, f32[256,128]{1,0:T(8,128)}) custom-call(s32[32]{0:T(128)} %dest_s.1, s32[1,32]{1,0:T(1,128)} %bitcast.23, s32[1,32]{1,0:T(1,128)} %bitcast.25, s32[32,1]{1,0:T(8,128)} %copy.16.clus_c, bf16[32,72,896]{2,1,0:T(8,128)(2,1)} %roll.1), custom_call_target="tpu_custom_call" | custom-call | tf_op jit(solution)/shard_map/pallas_call | solution.py:433
  141.0 59.8 %shard_map.147 = (bf16[32,72,896]{2,1,0:T(8,128)(2,1)}, f32[256,128]{1,0:T(8,128)}, bf16[4,768,896]{2,1,0:T(8,128)(2,1)}) custom-call(bf16[32,72,896]{2,1,0:T(8,128)(2,1)} %get-tuple-element.22.send, f32[256,128]{1,0:T(8,128)} %get-tuple-element.23.meta, bf16[768,896]{1,0:T(8,128)(2,1)} %lpg.1), custom_call_target="tpu_custom_call" | custom-call | tf_op jit(solution)/shard_map/pallas_call | solution.py:439
  200.8 10.7 %shard_map.148 = (bf16[768,896]{1,0:T(8,128)(2,1)}, bf16[768,896]{1,0:T(8,128)(2,1)}, f32[8,768]{1,0:T(8,128)}, f32[768,256]{1,0:T(8,128)}, f32[768,128]{1,0:T(8,128)}, /*index=5*/f32[768,128]{1,0:T(8,128)}) custom-call(bf16[2304,896]{1,0:T(8,128)(2,1)} %bitcast.21, f32[256,128]{1,0:T(8,128)} %get-tuple-element.25.meta, s32[32,1]{1,0:T(8,128)} %copy.17.len_c, ...), custom_call_target="tpu_custom_call" | custom-call | tf_op jit(solution)/shard_map/pallas_call | solution.py:445
  211.5 0.0 slice-start
  211.5 51.6 %shard_map.149 = (bf16[4,768,896]{2,1,0:T(8,128)(2,1)}, f32[4,8,768]{2,1,0:T(8,128)}) custom-call(bf16[768,896]{1,0:T(8,128)(2,1)} %get-tuple-element.26.own, f32[8,768]{1,0:T(8,128)} %get-tuple-element.27.sq), custom_call_target="tpu_custom_call" | custom-call | tf_op jit(solution)/shard_map/pallas_call | solution.py:452
  263.1 0.0 all-gather.2.cloned.1.call-done
  263.1 0.0 slice-start.1
  263.1 26.5 %shard_map.150 = (bf16[768,768]{1,0:T(8,128)(2,1)}, bf16[768,512]{1,0:T(8,128)(2,1)}, f32[768,128]{1,0:T(8,128)}, f32[8,768]{1,0:T(8,128)}) custom-call(bf16[4,768,896]{2,1,0:T(8,128)(2,1)} %get-tuple-element.28.xf, bf16[4,768,896]{2,1,0:T(8,128)(2,1)} %get-tuple-element.29.cf, bf16[4,896,1280]{2,1,0:T(8,128)(2,1)} %bitcast.16, ...), custom_call_target="tpu_custom_call" | custom-call | tf_op jit(solution)/shard_map/pallas_call | solution.py:458
  289.6 0.0 slice-done
  289.6 0.0 slice-done.1
  289.6 0.0 copy-start
  289.6 0.0 copy-start.1
  289.6 4.6 %convolution_convert_fusion.1 = bf16[4,896,512]{2,1,0:T(8,128)(2,1)S(1)} fusion(bf16[4,768,896]{2,1,0:T(8,128)(2,1)S(1)} %bitcast.19, bf16[768,512]{1,0:T(8,128)(2,1)} %get-tuple-element.38), kind=kOutput, calls=%fused_computation.2 | convolution fusion | flops 2820407296 | bytes 9961472 | tf_op jit(solution)/shard_map/dot_general | solution.py:472
  294.2 0.0 copy-done
  294.2 0.0 copy-done.1
  294.2 4.8 %convolution_convert_fusion = bf16[4,896,768]{2,1,0:T(8,128)(2,1)S(1)} fusion(bf16[4,768,896]{2,1,0:T(8,128)(2,1)S(1)} %copy-done, bf16[768,768]{1,0:T(8,128)(2,1)S(1)} %copy-done.1), kind=kOutput, calls=%fused_computation.1 | convolution fusion | flops 4230610944 | bytes 12189696 | tf_op jit(solution)/shard_map/dot_general | solution.py:472
  299.1 4.0 pad_maximum_fusion
  303.0 0.0 reduce-scatter.2.cloned.1.call-update
  303.0 54.0 %shard_map.151 = bf16[768,896]{1,0:T(8,128)(2,1)} custom-call(bf16[768,768]{1,0:T(8,128)(2,1)} %get-tuple-element.34.grads, bf16[4,896,1280]{2,1,0:T(8,128)(2,1)} %bitcast.17, f32[8,768]{1,0:T(8,128)} %get-tuple-element.35.dots, bf16[768,896]{1,0:T(8,128)(2,1)} %get-tuple-element.36.packed, bf16[768,896]{1,0:T(8,128)(2,1)} %lpg.1, ...), custom_call_target="tpu_custom_call" | custom-call | tf_op jit(solution)/shard_map/pallas_call | solution.py:477
  357.1 40.1 %reduce-scatter.2.cloned.1.call-done = bf16[112,1280]{1,0:T(8,128)(2,1)} async-done(((bf16[3584,1280]{1,0:T(8,128)(2,1)}), bf16[112,1280]{1,0:T(8,128)(2,1)}) %reduce-scatter.2.cloned.1.call-update) | async-done | bytes 286736 | tf_op jit(solution)/shard_map/reduce_scatter | solution.py:475
  397.2 1.7 fusion.2
  398.9 1.4 fusion.3
  400.2 2.5 copy.23
  (1 shorter events, 0.0 us)
Async XLA Ops:
  7.2 255.9 %all-gather.2.cloned.1.call-start = ((), (), s32[]{:S(2)}) async-start(), calls=%async_computation.1 | async-start | bytes 9461760 | tf_op jit(solution)/shard_map/all_gather | solution.py:430
  9.0 388.2 %reduce-scatter.2.cloned.1.call-start = ((), (), s32[]{:S(2)}) async-start(), calls=%async_computation.2 | async-start | bytes 9461760 | tf_op jit(solution)/shard_map/reduce_scatter | solution.py:475
  211.5 78.1 %slice-start = ((s8[5505024]{0:T(1024)(128)(4,1)}), s8[1310720]{0:T(1024)(128)(4,1)S(1)}, s32[]{:S(2)}) async-start(s8[5505024]{0:T(1024)(128)(4,1)} %bitcast.18), calls=%async_computation.3 | async-start | bytes 2621440
  263.1 26.5 %slice-start.1 = ((s8[5505024]{0:T(1024)(128)(4,1)}), s8[4194304]{0:T(1024)(128)(4,1)S(1)}, s32[]{:S(2)}) async-start(s8[5505024]{0:T(1024)(128)(4,1)} %bitcast.18), calls=%async_computation.4 | async-start | bytes 8388608
  289.6 4.6 %copy-start = (bf16[4,768,896]{2,1,0:T(8,128)(2,1)S(1)}, bf16[4,768,896]{2,1,0:T(8,128)(2,1)}, u32[]{:S(2)}) copy-start(bf16[4,768,896]{2,1,0:T(8,128)(2,1)} %get-tuple-element.28.xf) | copy-start | bytes 16515076
  289.6 4.6 %copy-start.1 = (bf16[768,768]{1,0:T(8,128)(2,1)S(1)}, bf16[768,768]{1,0:T(8,128)(2,1)}, u32[]{:S(2)}) copy-start(bf16[768,768]{1,0:T(8,128)(2,1)} %get-tuple-element.34.grads) | copy-start | bytes 3538948
Sparse Core Ops, SparseCore 0:
  10.3 58.3 all-gather.1
  303.2 93.9 reduce-scatter.1

commit v2 on v1

--- a/solution.py
+++ b/solution.py
@@ -52,16 +52,20 @@
     return lax.broadcasted_iota(jnp.int32, shape, dim)
 
 
-def stage_kernel(dest_s, dest_r, clus_r, clus_c, roll, send, meta, sem):
+def diagonal(row, n):
+    return jnp.sum(jnp.where(iota((n, n), 0) == iota((n, n), 1), row, 0.0), axis=1, keepdims=True)
+
+
+def stage_kernel(dest_s, dest_r, clus_r, roll, send, meta, sem):
     def start(s, c):
         t = dest_s[s] // SEQ
         pltpu.make_async_copy(roll.at[s], send.at[t], sem.at[s]).start()
         return c
 
     lax.fori_loop(0, SEQ, start, 0)
-    same = (clus_c[...] == clus_r[...]) & (iota((SEQ, SEQ), 0) // GSIZE == iota((SEQ, SEQ), 1) // GSIZE)
+    clus = clus_r[...].astype(F32)
     group = iota((SEQ, SEQ), 0) // GSIZE == iota((SEQ, SEQ), 1) // GSIZE
-    same = jnp.where(same, 1.0 / GSIZE, 0.0)
+    same = jnp.where((diagonal(clus, SEQ) == clus) & group, 1.0 / GSIZE, 0.0)
     share_c = jnp.sum(same, axis=1, keepdims=True)
     share_r = jnp.sum(same, axis=0, keepdims=True)
     mean_r = jnp.sum(jnp.where(group, share_c, 0.0), axis=0, keepdims=True) * (1.0 / GSIZE)
@@ -127,8 +131,7 @@
         pl.semaphore_signal(barrier, inc=1, device_id={"tp": lax.rem(z + d, N_Z)}, device_id_type=MESH)
     pl.semaphore_wait(barrier, len(OFFSETS) + 2)
     mine = [pltpu.make_async_copy(send.at[me], out.at[me], lsem.at[0]),
-            pltpu.make_async_copy(meta.at[pl.ds(8 * me, 8)], meta_out.at[pl.ds(8 * me, 8)], lsem.at[1]),
-            pltpu.make_async_copy(cot, cot_full.at[z], lsem.at[2])]
+            pltpu.make_async_copy(meta.at[pl.ds(8 * me, 8)], meta_out.at[pl.ds(8 * me, 8)], lsem.at[1])]
     ring = ring_start(cot, cot_full, z, zs, zr)
 
     def slab(i, frm, to, who):
@@ -158,10 +161,12 @@
         m.wait()
 
 
-def pack_kernel(rows, meta, len_c, gain, table, packed, scaled, squares, rope, pos_b, adv_b, keys):
+def pack_kernel(rows, meta, len_r, gain, table, packed, scaled, squares, rope, pos_b, adv_b, keys):
     lane = iota((SEQ, 128), 1)
     sub = iota((SEQ, 128), 0)
-    lens = len_c[...].astype(F32)
+    lens = diagonal(len_r[...].astype(F32), SEQ)
+    at_own = pl.ds(pl.multiple_of(lax.axis_index("tp") * FB, 128), FB)
+    gain_own = gain[:, at_own].astype(F32)
     ends = jnp.sum(jnp.where(sub <= lane, lens, 0.0), axis=0, keepdims=True)
     starts = jnp.sum(jnp.where(sub < lane, lens, 0.0), axis=0, keepdims=True)
     place = meta[pl.ds(0, SEQ, 8), :]
@@ -192,7 +197,7 @@
         pick = jnp.where(seg * 128.0 + pos[:, :1] == keys[...], 1.0, 0.0).astype(BF)
         took = nn(pick, rows[...])
         packed[at, :] = took.astype(BF)
-        scaled[at, :] = (took * gain[...].astype(F32)).astype(BF)
+        scaled[at, :] = (took * gain_own).astype(BF)
         square = jnp.sum(took * took, axis=1, keepdims=True)
         squares[:, at] = jnp.transpose(jnp.broadcast_to(square, (TB, 128)))[:8, :]
         return c
@@ -206,7 +211,7 @@
     for d in (1, 2, 3):
         pl.semaphore_signal(barrier, inc=1, device_id={"tp": lax.rem(z + d, N_Z)}, device_id_type=MESH)
     pl.semaphore_wait(barrier, 3)
-    mine = [pltpu.make_async_copy(own, full.at[z], lsem.at[0]), pltpu.make_async_copy(sq, sq_full.at[z], lsem.at[1])]
+    mine = [pltpu.make_async_copy(sq, sq_full.at[z], lsem.at[0])]
     ring = ring_start(own, full, z, zs, zr)
 
     def note(d, blk):
@@ -242,14 +247,19 @@
     return v * cos - jnp.concatenate([v[:, HD // 2:], v[:, :HD // 2]], axis=1) * sin
 
 
-def block_kernel(xf, cf, wf, sq, rope, pos_b, adv_b, grads, outs, inv_b, dots,
+def block_kernel(own_x, own_c, xf, cf, wf, sq, rope, pos_b, adv_b, grads, outs, inv_b, dots,
                  xv, cv, wv, sem, lin, ga, qrot, kbuf, vbuf, gab, dk, dv, mq):
-    copies = []
-    for b in range(N_Z):
-        copies.append([pltpu.make_async_copy(xf.at[b], xv.at[b], sem.at[b, 0]),
-                       pltpu.make_async_copy(cf.at[b], cv.at[b], sem.at[b, 1]),
-                       pltpu.make_async_copy(wf.at[b], wv.at[b], sem.at[b, 2])])
-        for k in copies[-1]:
+    z = lax.axis_index("tp")
+
+    def loads(d):
+        blk = lax.rem(z + d, N_Z)
+        first = isinstance(d, int) and d == 0
+        return [pltpu.make_async_copy(own_x if first else xf.at[blk], xv.at[d], sem.at[d, 0]),
+                pltpu.make_async_copy(own_c if first else cf.at[blk], cv.at[d], sem.at[d, 1]),
+                pltpu.make_async_copy(wf.at[blk], wv.at[d], sem.at[d, 2])]
+
+    for d in range(N_Z):
+        for k in loads(d):
             k.start()
     total = sq[0] + sq[1] + sq[2] + sq[3]
     inv_t = lax.rsqrt(total * (1.0 / D) + NORM_EPSILON)
@@ -261,14 +271,14 @@
     dv[...] = jnp.zeros_like(dv)
     lin[...] = jnp.zeros_like(lin)
     ga[...] = jnp.zeros_like(ga)
-    for b in range(N_Z):
-        for k in copies[b]:
+
+    def project(d, c):
+        for k in loads(d):
             k.wait()
-    def project(b, c):
         for n in range(3):
-            lin[:, n * 256:(n + 1) * 256] += nn(xv[b], wv[b, :, n * 256:(n + 1) * 256])
+            lin[:, n * 256:(n + 1) * 256] += nn(xv[d], wv[d, :, n * 256:(n + 1) * 256])
         for n in range(2):
-            ga[:, n * 256:(n + 1) * 256] += nn(cv[b], wv[b, :, 768 + n * 256:768 + (n + 1) * 256])
+            ga[:, n * 256:(n + 1) * 256] += nn(cv[d], wv[d, :, 768 + n * 256:768 + (n + 1) * 256])
         return c
 
     lax.fori_loop(0, N_Z, project, 0)
@@ -336,77 +346,176 @@
     lax.fori_loop(0, TOK // TB, finish, 0)
 
 
-def input_kernel(grads, wf, dots, packed, lpg, gain, inv_b, adv_b, result,
-                 wv, dots_all, sbuf, rbuf, own, wsem, zs, zr, ds_, dr):
+def grad_kernel(grads, outs, own_x, own_c, xf, cf, wf, dots, packed, gain, inv_b, adv_b,
+                result, res_q, res_k, res_v, res_o,
+                wv, xv, cv, dots_all, sbuf, rbuf, dw, pair, r1, s1, r2, s2, fin,
+                wsem, zs, zr, ds_, dr, ps, pr, s1s, s1r, s2s, s2r, fs, fr):
     z = lax.axis_index("tp")
+    me = lax.axis_index("fsdp")
+    y, x, c = me // 8, (me // 2) % 4, me % 2
     right, left, far = lax.rem(z + 1, N_Z), lax.rem(z + 3, N_Z), lax.rem(z + 2, N_Z)
+    other = 1 - c
+    sib = {"fsdp": y * 8 + x * 2 + other}
+    width = QC + 2 * KC
+
+    def on_x(d):
+        return {"fsdp": y * 8 + lax.rem(x + d, 4) * 2 + c}
+
+    def on_y(d):
+        return {"fsdp": lax.rem(y + d, 4) * 8 + x * 2 + c}
+
     order = [far, right, left, z]
-    loads = [pltpu.make_async_copy(wf.at[t, :, pl.ds(0, QC + 2 * KC)], wv.at[i], wsem.at[i]) for i, t in enumerate(order)]
-    for k in loads:
+    wl = [pltpu.make_async_copy(wf.at[t, :, pl.ds(0, width)], wv.at[i], wsem.at[i, 0]) for i, t in enumerate(order)]
+    for k in wl:
+        k.start()
+    rows = [pltpu.make_async_copy(own_x, xv.at[z], wsem.at[0, 1]), pltpu.make_async_copy(own_c, cv.at[z], wsem.at[0, 2])]
+    for d in (1, 2, 3):
+        t = lax.rem(z + d, N_Z)
+        rows += [pltpu.make_async_copy(xf.at[t], xv.at[t], wsem.at[d, 1]),
+                 pltpu.make_async_copy(cf.at[t], cv.at[t], wsem.at[d, 2])]
+    for k in rows:
         k.start()
     barrier = pltpu.get_barrier_semaphore()
     for d in (1, 2, 3):
-        pl.semaphore_signal(barrier, inc=1, device_id={"tp": lax.rem(z + d, N_Z)}, device_id_type=MESH)
-    pl.semaphore_wait(barrier, 3)
-
-    def note(d, blk):
+        for who in ({"tp": lax.rem(z + d, N_Z)}, on_x(d), on_y(d)):
+            pl.semaphore_signal(barrier, inc=1, device_id=who, device_id_type=MESH)
+    pl.semaphore_signal(barrier, inc=1, device_id=sib, device_id_type=MESH)
+    pl.semaphore_wait(barrier, 10)
+
+    def remote(src, dst, ss, rs, who):
         return pltpu.make_async_remote_copy(
-            src_ref=dots, dst_ref=dots_all.at[d - 1], send_sem=ds_.at[d], recv_sem=dr.at[d],
-            device_id={"tp": lax.rem(z + d, N_Z)}, device_id_type=MESH)
-
-    for d in (1, 2, 3):
-        note(d, z).start()
-
-    def ship(i, to):
-        return pltpu.make_async_remote_copy(
-            src_ref=sbuf.at[i], dst_ref=rbuf.at[i], send_sem=zs.at[i], recv_sem=zr.at[i],
-            device_id={"tp": to}, device_id_type=MESH)
+            src_ref=src, dst_ref=dst, send_sem=ss, recv_sem=rs, device_id=who, device_id_type=MESH)
+
+    def note(d):
+        return remote(dots, dots_all.at[d - 1], ds_.at[d], dr.at[d], {"tp": lax.rem(z + d, N_Z)})
+
+    for d in (1, 2, 3):
+        note(d).start()
+
+    def ship(i):
+        return remote(sbuf.at[i], rbuf.at[i], zs.at[i], zr.at[i], {"tp": right if i % 2 == 0 else left})
 
     def share(i, h):
         return nt(grads[h * HALF:(h + 1) * HALF, :], wv[i])
 
-    loads[0].wait()
-    sbuf[0] = share(0, 0).astype(BF)
-    ship(0, right).start()
-    sbuf[1] = share(0, 1).astype(BF)
-    ship(1, left).start()
-    loads[1].wait()
-    sbuf[2] = share(1, 1).astype(BF)
-    ship(2, right).start()
-    loads[2].wait()
-    sbuf[3] = share(2, 0).astype(BF)
-    ship(3, left).start()
-    a = share(1, 0)
-    ship(0, right).wait_recv()
-    sbuf[4] = (a + rbuf[0].astype(F32)).astype(BF)
-    ship(4, right).start()
-    a = share(2, 1)
-    ship(1, left).wait_recv()
-    sbuf[5] = (a + rbuf[1].astype(F32)).astype(BF)
-    ship(5, left).start()
-    loads[3].wait()
-    own[:HALF] = share(3, 0)
-    own[HALF:] = share(3, 1)
-    for d in (1, 2, 3):
-        note(d, z).wait_recv()
-        note(d, z).wait_send()
+    for i, (w, h) in enumerate([(0, 0), (0, 1), (1, 1), (2, 0)]):
+        if i != 1:
+            wl[w].wait()
+        sbuf[i] = share(w, h).astype(BF)
+        ship(i).start()
+    for k in rows:
+        k.wait()
+
+    def swap(i):
+        b = lax.rem(y + 1 + i, 4)
+        return remote(dw.at[other, b], pair.at[b], ps.at[i], pr.at[i], sib)
+
+    def terms(i, carry):
+        b = lax.rem(y + 1 + i, 4)
+        lo = tn(xv[b], grads[:, :QC + KC]).astype(BF)
+        mid = tn(xv[b], grads[:, QC + KC:]).astype(BF)
+        hi = tn(cv[b], outs[...]).astype(BF)
+        for j in range(8):
+            at = slice(112 * j, 112 * (j + 1))
+            dw[0, b, j // 2, j % 2] = lo[at]
+            dw[1, b, j // 2, j % 2, :, :KC] = mid[at]
+            dw[1, b, j // 2, j % 2, :, KC:] = hi[at]
+        swap(i).start()
+        return carry
+
+    lax.fori_loop(0, 4, terms, 0)
+    for i, w in ((4, 1), (5, 2)):
+        a = share(w, i % 2)
+        ship(i - 4).wait_recv()
+        sbuf[i] = (a + rbuf[i - 4].astype(F32)).astype(BF)
+        ship(i).start()
+
+    def hop_y(d):
+        return remote(dw.at[c, lax.rem(y + d, 4), :, 1], r1.at[1, d - 1], s1s.at[1, d - 1], s1r.at[1, d - 1], on_y(d))
+
+    def hop_x(d):
+        return remote(dw.at[c, :, lax.rem(x + d, 4), 0], r1.at[0, d - 1], s1s.at[0, d - 1], s1r.at[0, d - 1], on_x(d))
+
+    def chip_sum(i, carry):
+        b = lax.rem(y + 1 + i, 4)
+        swap(i).wait_recv()
+        for j in range(4):
+            dw[c, b, j] = (dw[c, b, j].astype(F32) + pair[b, j].astype(F32)).astype(BF)
+
+        @pl.when(i < 3)
+        def _():
+            hop_y(i + 1).start()
+
+        return carry
+
+    lax.fori_loop(0, 4, chip_sum, 0)
+    for d in (1, 2, 3):
+        hop_x(d).start()
+    wl[3].wait()
+    own = share(3, 0)
+    sbuf[6] = own.astype(BF)
+    own = share(3, 1)
+    sbuf[7] = own.astype(BF)
+    for d in (1, 2, 3):
+        note(d).wait()
     m = (dots[...] + dots_all[0] + dots_all[1] + dots_all[2]) * (1.0 / D)
-    ship(2, right).wait_recv()
-    ship(3, left).wait_recv()
-    ship(4, right).wait_recv()
-    ship(5, left).wait_recv()
+
+    for d in (1, 2, 3):
+        hop_y(d).wait_recv()
+        hop_x(d).wait_recv()
+    for j in range(4):
+        s1[1, j] = (dw[c, y, j, 1].astype(F32) + r1[1, 0, j].astype(F32) + r1[1, 1, j].astype(F32)
+                    + r1[1, 2, j].astype(F32)).astype(BF)
+        s1[0, j] = (dw[c, j, x, 0].astype(F32) + r1[0, 0, j].astype(F32) + r1[0, 1, j].astype(F32)
+                    + r1[0, 2, j].astype(F32)).astype(BF)
+
+    def last_x(d):
+        return remote(s1.at[1, lax.rem(x + d, 4)], r2.at[1, d - 1], s2s.at[1, d - 1], s2r.at[1, d - 1], on_x(d))
+
+    def last_y(d):
+        return remote(s1.at[0, lax.rem(y + d, 4)], r2.at[0, d - 1], s2s.at[0, d - 1], s2r.at[0, d - 1], on_y(d))
+
+    for d in (1, 2, 3):
+        last_x(d).start()
+        last_y(d).start()
+    for d in (1, 2, 3):
+        last_x(d).wait_recv()
+        last_y(d).wait_recv()
+    for p, own in ((0, s1[0, y]), (1, s1[1, x])):
+        s2[p] = (own.astype(F32) + r2[p, 0].astype(F32) + r2[p, 1].astype(F32) + r2[p, 2].astype(F32)).astype(BF)
+    trade = remote(s2.at[other], fin.at[c], fs.at[0], fr.at[0], sib)
+    trade.start()
+    for i in (2, 3, 4, 5):
+        ship(i).wait_recv()
+    gain_own = gain[:, pl.ds(pl.multiple_of(z * FB, 128), FB)].astype(F32)
     for b in range(TOK // TB):
         h, r = divmod(b * TB, HALF)
         at = slice(b * TB, (b + 1) * TB)
         hs = slice(r, r + TB)
         one, two = (4, 3) if h == 0 else (2, 5)
-        s = own[at, :] + rbuf[one, hs, :].astype(F32) + rbuf[two, hs, :].astype(F32)
+        s = sbuf[6 + h, hs, :].astype(F32) + rbuf[one, hs, :].astype(F32) + rbuf[two, hs, :].astype(F32)
         mc = jnp.transpose(jnp.broadcast_to(m[:1, at], (128, TB)))[:, :1]
         inv = inv_b[at, :1]
-        result[at, :] = (adv_b[at, :1] * lpg[at, :].astype(F32) + s * gain[...].astype(F32)
+        result[at, :] = (adv_b[at, :1] * cv[z, at, :].astype(F32) + s * gain_own
                          - packed[at, :].astype(F32) * (inv * mc)).astype(BF)
+    trade.wait()
+    mine = s2[c]
+    got = fin[other]
+    low = jnp.where(c == 0, mine, got)
+    high = jnp.where(c == 0, got, mine)
+    res_q[...] = low[:, :QC]
+    res_k[...] = low[:, QC:]
+    res_v[...] = high[:, :KC]
+    res_o[...] = high[:, KC:]
     for i in range(6):
-        ship(i, right if i % 2 == 0 else left).wait_send()
+        ship(i).wait_send()
+    for i in range(4):
+        swap(i).wait_send()
+    for d in (1, 2, 3):
+        hop_x(d).wait_send()
+        hop_y(d).wait_send()
+        last_x(d).wait_send()
+        last_y(d).wait_send()
 
 
 def sds(shape, dtype=BF):
@@ -426,20 +535,19 @@
 
 
 def per_device(roll_rows, dest, lengths, clusters, log_prob_grad, gain, w_q, w_k, w_v, w_o_t):
-    z = lax.axis_index("tp")
     weights = lax.all_gather(jnp.concatenate([w_q, w_k, w_v, w_o_t], axis=1), "fsdp", axis=0, tiled=True)
     weights = weights.reshape(N_Z, FB, QC * 2 + KC * 2)
-    gain_own = lax.dynamic_slice(gain, (z * FB,), (FB,)).reshape(1, FB)
+    gain = gain.reshape(1, D)
     send, meta = pl.pallas_call(
         stage_kernel, out_shape=(sds((SEQ, MAXLEN, FB)), sds((SEQ * 8, 128), F32)),
-        in_specs=[SMEM, VMEM, VMEM, VMEM, HBM], out_specs=(HBM, VMEM),
+        in_specs=[SMEM, VMEM, VMEM, HBM], out_specs=(VMEM, VMEM),
         scratch_shapes=[DMA((SEQ,))], compiler_params=params(),
-    )(dest, dest.reshape(1, SEQ), clusters.reshape(1, SEQ), clusters.reshape(SEQ, 1), roll_rows)
+    )(dest, dest.reshape(1, SEQ), clusters.reshape(1, SEQ), roll_rows)
     n_o = len(OFFSETS)
     arrived, meta_in, cot = pl.pallas_call(
         hand_kernel, out_shape=(sds((SEQ, MAXLEN, FB)), sds((SEQ * 8, 128), F32), sds((N_Z, TOK, FB))),
         in_specs=[HBM, HBM, HBM], out_specs=(HBM, HBM, HBM),
-        scratch_shapes=[DMA((3,)), DMA((n_o,)), DMA((n_o,)), DMA((n_o,)), DMA((n_o,)), DMA((6,)), DMA((6,))],
+        scratch_shapes=[DMA((2,)), DMA((n_o,)), DMA((n_o,)), DMA((n_o,)), DMA((n_o,)), DMA((6,)), DMA((6,))],
         compiler_params=params(collective_id=0),
     )(send, meta, log_prob_grad)
     packed, scaled, squares, rope, pos_b, adv_b = pl.pallas_call(
@@ -448,43 +556,42 @@
                    sds((TOK, 128), F32), sds((TOK, 128), F32)),
         in_specs=[VMEM] * 5, out_specs=(VMEM,) * 6,
         scratch_shapes=[pltpu.VMEM((1, SEQ * MAXLEN), F32)], compiler_params=params(),
-    )(arrived.reshape(SEQ * MAXLEN, FB), meta_in, lengths.reshape(SEQ, 1), gain_own, jnp.asarray(rope_table()))
+    )(arrived.reshape(SEQ * MAXLEN, FB), meta_in, lengths, gain, jnp.asarray(rope_table()))
     rows, sq = pl.pallas_call(
         gather_kernel, out_shape=(sds((N_Z, TOK, FB)), sds((N_Z, 8, TOK), F32)),
         in_specs=[HBM, HBM], out_specs=(HBM, HBM),
-        scratch_shapes=[DMA((2,)), DMA((6,)), DMA((6,)), DMA((4,)), DMA((4,))],
+        scratch_shapes=[DMA((1,)), DMA((6,)), DMA((6,)), DMA((4,)), DMA((4,))],
         compiler_params=params(collective_id=1),
     )(scaled, squares)
+    width = QC + 2 * KC
     grads, outs, inv_b, dots = pl.pallas_call(
         block_kernel,
-        out_shape=(sds((TOK, QC + 2 * KC)), sds((TOK, QC)), sds((TOK, 128), F32), sds((8, TOK), F32)),
-        in_specs=[HBM, HBM, HBM] + [VMEM] * 4, out_specs=(VMEM,) * 4,
+        out_shape=(sds((TOK, width)), sds((TOK, QC)), sds((TOK, 128), F32), sds((8, TOK), F32)),
+        in_specs=[HBM] * 5 + [VMEM] * 4, out_specs=(VMEM,) * 4,
         scratch_shapes=[
             pltpu.VMEM((N_Z, TOK, FB), BF), pltpu.VMEM((N_Z, TOK, FB), BF),
-            pltpu.VMEM((N_Z, FB, 2 * QC + 2 * KC), BF), DMA((N_Z, 3)),
-            pltpu.VMEM((TOK, QC + 2 * KC), F32), pltpu.VMEM((TOK, QC), F32),
+            pltpu.VMEM((N_Z, FB, width + QC), BF), DMA((N_Z, 3)),
+            pltpu.VMEM((TOK, width), F32), pltpu.VMEM((TOK, QC), F32),
             pltpu.VMEM((TOK, QC), BF), pltpu.VMEM((TOK + TB, HD), BF), pltpu.VMEM((TOK + TB, HD), BF),
             pltpu.VMEM((TOK, QC), BF), pltpu.VMEM((TOK + TB, HD), F32), pltpu.VMEM((TOK + TB, HD), F32),
             pltpu.VMEM((TOK, HD), F32)],
         compiler_params=params(),
-    )(rows, cot, weights, sq, rope, pos_b, adv_b)
-    def terms(left, right):
-        t = lax.dot_general(left, right, (((1,), (0,)), ((), ())), preferred_element_type=F32)
-        return t.astype(BF).reshape(D, right.shape[1])
-
-    total = lax.psum_scatter(
-        jnp.concatenate([terms(rows, grads), terms(cot, outs)], axis=1), "fsdp", scatter_dimension=0, tiled=True)
-    input_grad = pl.pallas_call(
-        input_kernel, out_shape=sds((TOK, FB)),
-        in_specs=[VMEM, HBM] + [VMEM] * 6, out_specs=VMEM,
+    )(scaled, log_prob_grad, rows, cot, weights, sq, rope, pos_b, adv_b)
+    half = (112, QC + KC)
+    return pl.pallas_call(
+        grad_kernel,
+        out_shape=(sds((TOK, FB)), sds((112, QC)), sds((112, KC)), sds((112, KC)), sds((112, QC))),
+        in_specs=[VMEM, VMEM] + [HBM] * 5 + [VMEM] * 5, out_specs=(VMEM,) * 5,
         scratch_shapes=[
-            pltpu.VMEM((N_Z, FB, QC + 2 * KC), BF), pltpu.VMEM((3, 8, TOK), F32),
-            pltpu.VMEM((6, HALF, FB), BF), pltpu.VMEM((6, HALF, FB), BF), pltpu.VMEM((TOK, FB), F32),
-            DMA((N_Z,)), DMA((6,)), DMA((6,)), DMA((4,)), DMA((4,))],
+            pltpu.VMEM((N_Z, FB, width), BF), pltpu.VMEM((N_Z, TOK, FB), BF), pltpu.VMEM((N_Z, TOK, FB), BF),
+            pltpu.VMEM((3, 8, TOK), F32), pltpu.VMEM((8, HALF, FB), BF), pltpu.VMEM((6, HALF, FB), BF),
+            pltpu.VMEM((2, 4, 4, 2) + half, BF), pltpu.VMEM((4, 4, 2) + half, BF),
+            pltpu.VMEM((2, 3, 4) + half, BF), pltpu.VMEM((2, 4) + half, BF), pltpu.VMEM((2, 3) + half, BF),
+            pltpu.VMEM((2,) + half, BF), pltpu.VMEM((2,) + half, BF),
+            DMA((N_Z, 3)), DMA((6,)), DMA((6,)), DMA((4,)), DMA((4,)), DMA((4,)), DMA((4,)),
+            DMA((2, 3)), DMA((2, 3)), DMA((2, 3)), DMA((2, 3)), DMA((1,)), DMA((1,))],
         compiler_params=params(collective_id=2),
-    )(grads, weights, dots, packed, log_prob_grad, gain_own, inv_b, adv_b)
-    a, b, c = QC, QC + KC, QC + 2 * KC
-    return (input_grad, total[:, :a], total[:, a:b], total[:, b:c], total[:, c:])
+    )(grads, outs, scaled, log_prob_grad, rows, cot, weights, dots, packed, gain, inv_b, adv_b)
 
 
 def solution(mesh):

time: 411 us -> 251 us (0.61)
  Pallas kernels: 330 us -> 225 us
  waiting for transfers between devices: 40.2 us -> 0.04 us
  matrix products: 9.4 us -> 0 us
    pallas_call x1, Pallas kernels: 128 us -> 5.31 us  [per_device(): pl.pallas_call(stage_kernel, out_shape=(sds((SEQ, MAXLEN, FB)), sds((SEQ...]
    reduce_scatter x1 -> x0, waiting for transfers between devices: 40.1 us -> none  [per_device(): lax.psum_scatter(jnp.concatenate([terms(rows, grads), terms(cot, outs)],...]
    pallas_call x2, Pallas kernels: 80.5 us -> 92.7 us  [the longest x1 71 us: per_device(): pl.pallas_call(grad_kernel, out_shape=(sds((TOK, FB)), sds((112, QC)), sd...]
    dot_general x2 -> x0, matrix products: 9.4 us -> none  [terms(): lax.dot_general(left, right, (((1,), (0,)), ((), ())), preferred_element_...]
    unnamed x9 -> x5, local copies, waits for them, and re-layouts: 2.54 us -> 8.34 us
    pallas_call x1, Pallas kernels: 59.8 us -> 64.5 us  [per_device(): pl.pallas_call(hand_kernel, out_shape=(sds((SEQ, MAXLEN, FB)), sds((SEQ *...]
  transfers between devices with their start and end apart: 2 -> 1, of which waited for: 1 -> 0; matrix products, arithmetic and copies ran while one was open for 1% -> 1% of each run, Pallas kernels for 74% -> 53%
where the time goes in v2:
time: 251 us
  Pallas kernels  225 us (90%)
  between operations  14.1 us (6%)
  local copies, waits for them, and re-layouts  9.65 us (4%)
    pallas_call x1, Pallas kernels, per_device(): pl.pallas_call(grad_kernel, out_shape=(sds((TOK, FB)), sds((112, QC)), sd...  71 us
    pallas_call x1, Pallas kernels, per_device(): pl.pallas_call(hand_kernel, out_shape=(sds((SEQ, MAXLEN, FB)), sds((SEQ *...  64.5 us
    pallas_call x1, Pallas kernels, per_device(): pl.pallas_call(gather_kernel, out_shape=(sds((N_Z, TOK, FB)), sds((N_Z, 8...  51.9 us
    pallas_call x1, Pallas kernels, per_device(): pl.pallas_call(block_kernel, out_shape=(sds((TOK, width)), sds((TOK, QC))...  21.8 us
    pallas_call x1, Pallas kernels, per_device(): pl.pallas_call(pack_kernel, out_shape=(sds((TOK, FB)), sds((TOK, FB)), sd...  10.7 us
    unnamed x5, local copies, waits for them, and re-layouts  8.34 us
    pallas_call x1, Pallas kernels, per_device(): pl.pallas_call(stage_kernel, out_shape=(sds((SEQ, MAXLEN, FB)), sds((SEQ...  5.31 us
  transfers between devices with their start and end apart: 1, of which 0 were waited for; matrix products, arithmetic and copies ran while one was open for 1% of the time, Pallas kernels for 53%

profile of v2, /device:TPU:1, one launch (start us, length us, event | category | flops | bytes accessed | tf_op | source)
XLA Modules:
  0.0 250.7 jit_solution(1974098351274987952)
XLA Ops:
  7.2 0.0 all-gather.2.cloned.1.call-start
  7.2 1.7 pad_maximum_fusion
  9.0 0.0 all-gather.2.cloned.1.call-update
  9.0 1.3 reshape.28.gain
  10.3 5.3 %shard_map.146 = (bf16[32,72,896]{2,1,0:T(8,128)(2,1)}, f32[256,128]{1,0:T(8,128)}) custom-call(s32[32]{0:T(128)} %dest_s.1, s32[1,32]{1,0:T(1,128)} %bitcast.7, s32[1,32]{1,0:T(1,128)} %bitcast.8, bf16[32,72,896]{2,1,0:T(8,128)(2,1)} %roll.1), custom_call_target="tpu_custom_call" | custom-call | tf_op jit(solution)/shard_map/pallas_call | solution.py:541
  15.6 64.5 %shard_map.147 = (bf16[32,72,896]{2,1,0:T(8,128)(2,1)}, f32[256,128]{1,0:T(8,128)}, bf16[4,768,896]{2,1,0:T(8,128)(2,1)}) custom-call(bf16[32,72,896]{2,1,0:T(8,128)(2,1)} %get-tuple-element.22.send, f32[256,128]{1,0:T(8,128)} %get-tuple-element.23.meta, bf16[768,896]{1,0:T(8,128)(2,1)} %own_c.3), custom_call_target="tpu_custom_call" | custom-call | tf_op jit(solution)/shard_map/pallas_call | solution.py:547
  80.1 10.7 %shard_map.148 = (bf16[768,896]{1,0:T(8,128)(2,1)}, bf16[768,896]{1,0:T(8,128)(2,1)}, f32[8,768]{1,0:T(8,128)}, f32[768,256]{1,0:T(8,128)}, f32[768,128]{1,0:T(8,128)}, /*index=5*/f32[768,128]{1,0:T(8,128)}) custom-call(bf16[2304,896]{1,0:T(8,128)(2,1)} %bitcast.6, f32[256,128]{1,0:T(8,128)} %get-tuple-element.25.meta, s32[1,32]{1,0:T(1,128)} %len_r.1, ...), custom_call_target="tpu_custom_call" | custom-call | tf_op jit(solution)/shard_map/pallas_call | solution.py:553
  90.9 51.9 %shard_map.149 = (bf16[4,768,896]{2,1,0:T(8,128)(2,1)}, f32[4,8,768]{2,1,0:T(8,128)}) custom-call(bf16[768,896]{1,0:T(8,128)(2,1)} %get-tuple-element.26.own.own_x, f32[8,768]{1,0:T(8,128)} %get-tuple-element.27.sq), custom_call_target="tpu_custom_call" | custom-call | tf_op jit(solution)/shard_map/pallas_call | solution.py:560
  142.7 0.0 all-gather.2.cloned.1.call-done
  142.8 21.8 %shard_map.150 = (bf16[768,768]{1,0:T(8,128)(2,1)}, bf16[768,512]{1,0:T(8,128)(2,1)}, f32[768,128]{1,0:T(8,128)}, f32[8,768]{1,0:T(8,128)}) custom-call(bf16[768,896]{1,0:T(8,128)(2,1)} %get-tuple-element.26.own.own_x, bf16[768,896]{1,0:T(8,128)(2,1)} %own_c.3, bf16[4,768,896]{2,1,0:T(8,128)(2,1)} %get-tuple-element.28.xf, ...), custom_call_target="tpu_custom_call" | custom-call | tf_op jit(solution)/shard_map/pallas_call | solution.py:567
  164.6 71.0 %shard_map.151 = (bf16[768,896]{1,0:T(8,128)(2,1)}, bf16[112,512]{1,0:T(8,128)(2,1)}, bf16[112,128]{1,0:T(8,128)(2,1)}, bf16[112,128]{1,0:T(8,128)(2,1)}, bf16[112,512]{1,0:T(8,128)(2,1)}) custom-call(bf16[768,768]{1,0:T(8,128)(2,1)} %get-tuple-element.34.grads, bf16[768,512]{1,0:T(8,128)(2,1)} %get-tuple-element.35.outs, ...), custom_call_target="tpu_custom_call" | custom-call | tf_op jit(solution)/shard_map/pallas_call | solution.py:581
  235.5 2.5 %copy.21 = bf16[768,896]{1,0:T(8,128)(2,1)} copy(bf16[768,896]{1,0:T(8,128)(2,1)} %get-tuple-element.44) | data formatting | bytes 2752512
  238.1 1.6 copy.22
  239.6 1.4 copy.23
  241.0 1.4 copy.24
  242.3 1.6 copy.25
Async XLA Ops:
  7.2 135.6 %all-gather.2.cloned.1.call-start = ((), (), s32[]{:S(2)}) async-start(), calls=%async_computation | async-start | bytes 9461760 | tf_op jit(solution)/shard_map/all_gather | solution.py:538
Sparse Core Ops, SparseCore 0:
  10.3 90.7 all-gather.1

commit v3 on v2

v3 whole, which is shorter than its diff:
```python
import jax
import jax.numpy as jnp
import numpy as np
from jax import lax
from jax.experimental import pallas as pl
from jax.experimental.pallas import tpu as pltpu
from jax.sharding import PartitionSpec as P

HD = 128
GSIZE = 16
ROPE_BASE = 1000000.0
NORM_EPSILON = 1e-06
MESH = pl.DeviceIdType.MESH
BF = jnp.bfloat16
F32 = jnp.float32
HBM = pl.BlockSpec(memory_space=pl.ANY)
VMEM = pl.BlockSpec(memory_space=pltpu.VMEM)
SMEM = pl.BlockSpec(memory_space=pltpu.SMEM)
DMA = pltpu.SemaphoreType.DMA
LIMIT = 60 * 2**20

N_F = 32
N_Z = 4
SEQ = 32
MAXLEN = 72
TOK = 768
HALF = TOK // 2
FB = 896
FA = 512
SLAB = 80
D = 3584
QC = 512
KC = 128
TB = 128

CHIPS = [(0, 1), (1, 0), (0, 3), (3, 0), (1, 1), (3, 3), (1, 3), (3, 1),
         (0, 2), (2, 0), (1, 2), (2, 1), (3, 2), (2, 3), (2, 2)]
OFFSETS = [(0, 0, 1)] + [(a, b, c) for c in range(2) for a, b in CHIPS]


def nt(a, b):
    return lax.dot_general(a, b, (((1,), (1,)), ((), ())), preferred_element_type=F32)


def tn(a, b):
    return lax.dot_general(a, b, (((0,), (0,)), ((), ())), preferred_element_type=F32)


def nn(a, b):
    return lax.dot_general(a, b, (((1,), (0,)), ((), ())), preferred_element_type=F32)


def iota(shape, dim):
    return lax.broadcasted_iota(jnp.int32, shape, dim)


def diagonal(row, n):
    return jnp.sum(jnp.where(iota((n, n), 0) == iota((n, n), 1), row, 0.0), axis=1, keepdims=True)


def stage_kernel(dest_s, dest_r, clus_r, roll, send_a, send_b, meta):
    def place(s, c):
        at = pl.ds(pl.multiple_of((dest_s[s] // SEQ) * SLAB, 16), SLAB)
        v = jnp.concatenate([roll[s], jnp.zeros((SLAB - MAXLEN, FB), BF)], axis=0)
        send_a[at, :] = v[:, :FA]
        send_b[at, :] = v[:, FA:]
        return c

    lax.fori_loop(0, SEQ, place, 0)
    clus = clus_r[...].astype(F32)
    group = iota((SEQ, SEQ), 0) // GSIZE == iota((SEQ, SEQ), 1) // GSIZE
    same = jnp.where((diagonal(clus, SEQ) == clus) & group, 1.0 / GSIZE, 0.0)
    share_c = jnp.sum(same, axis=1, keepdims=True)
    share_r = jnp.sum(same, axis=0, keepdims=True)
    mean_r = jnp.sum(jnp.where(group, share_c, 0.0), axis=0, keepdims=True) * (1.0 / GSIZE)
    adv_r = (share_r - mean_r).astype(BF).astype(F32)
    rows = iota((SEQ * 8, SEQ), 0)
    dest_v = dest_r[...]
    hit = dest_v // SEQ == rows // 8
    what = jnp.where(rows % 8 < 4, (dest_v % SEQ).astype(F32), adv_r)
    meta[...] = jnp.broadcast_to(jnp.sum(jnp.where(hit, what, 0.0), axis=1, keepdims=True), (SEQ * 8, 128))


def remote(src, dst, ss, rs, who):
    return pltpu.make_async_remote_copy(
        src_ref=src, dst_ref=dst, send_sem=ss, recv_sem=rs, device_id=who, device_id_type=MESH)


class Ring:
    def __init__(self, own, dst, cols, z, ss, rs):
        self.own, self.dst, self.cols, self.z, self.ss, self.rs = own, dst, cols, z, ss, rs
        self.right, self.left, self.far = (lax.rem(z + d, N_Z) for d in (1, 3, 2))

    def copy(self, i, blk, src=None):
        half = (0, 1, 1, 0, 0, 1)[i]
        at = pl.ds(half * HALF, HALF)
        to = self.right if i % 2 == 0 else self.left
        src = self.own if src is None else src
        return remote(src.at[at, self.cols], self.dst.at[blk, at, self.cols], self.ss.at[i], self.rs.at[i], {"tp": to})

    def start(self):
        for i in range(4):
            self.copy(i, self.z).start()

    def hand_on(self):
        for i, blk in ((0, self.left), (1, self.right)):
            self.copy(i, blk).wait_recv()
            self.copy(i + 4, blk, self.dst.at[blk]).start()

    def near(self):
        self.copy(2, self.left).wait_recv()
        self.copy(3, self.right).wait_recv()

    def end(self):
        self.copy(4, self.far).wait_recv()
        self.copy(5, self.far).wait_recv()

    def sent(self):
        for i in range(4):
            self.copy(i, self.z).wait_send()
        self.copy(4, self.left, self.dst.at[self.left]).wait_send()
        self.copy(5, self.right, self.dst.at[self.right]).wait_send()


def unstack(v):
    return jnp.concatenate([v[h * TB:(h + 1) * TB] for h in range(4)], axis=1)


def stack(v):
    return jnp.concatenate([v[:, h * HD:(h + 1) * HD] for h in range(4)], axis=0)


def turn(v, cos, sin):
    return v * cos + jnp.concatenate([v[:, HD // 2:], v[:, :HD // 2]], axis=1) * sin


def turn_back(v, cos, sin):
    return v * cos - jnp.concatenate([v[:, HD // 2:], v[:, :HD // 2]], axis=1) * sin


def front_kernel(send_a, send_b, meta, cot, len_r, gain, table, w_q, w_k, w_v, w_o,
                 x_out, c_out, w_out, packed, grads, outs, inv_b, adv_b, dots,
                 arr_a, arr_b, meta_in, pick, xv, cv, wsh, wv, sq, sq_all, sqc, rope, pos_b,
                 lin, ga, qrot, kbuf, vbuf, gab, dk, dv, mq,
                 lsem, osem, as_, ar, bs, br, ms, mr, zs, zr, us, ur, vs, vr, qs, qr,
                 w0s, w0r, w1s, w1r, w2s, w2r, w3s, w3r):
    me = lax.axis_index("fsdp")
    z = lax.axis_index("tp")
    y, x, c = me // 8, (me // 2) % 4, me % 2
    other = 1 - c
    sib = {"fsdp": y * 8 + x * 2 + other}

    def peer(o, s):
        return lax.rem(y + s * o[0] + 4, 4) * 8 + lax.rem(x + s * o[1] + 4, 4) * 2 + lax.rem(c + s * o[2] + 2, 2)

    def on_x(d):
        return {"fsdp": peer((0, d, 0), 1)}

    def on_y(d):
        return {"fsdp": peer((d, 0, 0), 1)}

    cot_own = pltpu.make_async_copy(cot, cv.at[z], lsem.at[0])
    cot_own.start()
    barrier = pltpu.get_barrier_semaphore()
    for o in OFFSETS:
        pl.semaphore_signal(barrier, inc=1, device_id={"fsdp": peer(o, 1)}, device_id_type=MESH)
    for d in (1, 2, 3):
        pl.semaphore_signal(barrier, inc=1, device_id={"tp": lax.rem(z + d, N_Z)}, device_id_type=MESH)
    pl.semaphore_wait(barrier, len(OFFSETS) + 3)

    ring_c = Ring(cot, cv, pl.ds(0, FB), z, zs, zr)
    ring_a = Ring(xv.at[z], xv, pl.ds(0, FA), z, us, ur)
    ring_b = Ring(xv.at[z], xv, pl.ds(FA, FB - FA), z, vs, vr)
    ring_c.start()

    def slab(k):
        return pl.ds(pl.multiple_of(k * SLAB, 16), SLAB)

    def eight(k):
        return pl.ds(pl.multiple_of(k * 8, 8), 8)

    def part_a(i, frm, to, who):
        return remote(send_a.at[slab(frm)], arr_a.at[slab(to)], as_.at[i], ar.at[i], {"fsdp": who})

    def part_b(i, frm, to, who):
        return remote(send_b.at[slab(frm)], arr_b.at[slab(to)], bs.at[i], br.at[i], {"fsdp": who})

    def note(i, frm, to, who):
        return remote(meta.at[eight(frm)], meta_in.at[eight(to)], ms.at[i], mr.at[i], {"fsdp": who})

    for kind in (note, part_a, part_b):
        for i, o in enumerate(OFFSETS):
            t = peer(o, 1)
            kind(i, t, me, t).start()
    mine = [pltpu.make_async_copy(send_a.at[slab(me)], arr_a.at[slab(me)], lsem.at[1]),
            pltpu.make_async_copy(send_b.at[slab(me)], arr_b.at[slab(me)], lsem.at[2]),
            pltpu.make_async_copy(meta.at[eight(me)], meta_in.at[eight(me)], lsem.at[3])]
    for k in mine:
        k.start()

    wsh[0, :, :QC] = w_q[...]
    wsh[0, :, QC:] = w_k[...]
    wsh[1, :, :KC] = w_v[...]
    wsh[1, :, KC:] = w_o[...]
    wv[0, y, x, c] = wsh[0]
    wv[1, y, x, c] = wsh[1]
    w_pair = remote(wsh.at[other], wv.at[other, y, x, c], w0s.at[0], w0r.at[0], sib)
    w_pair.start()

    def w_near(p, d):
        return remote(wv.at[c, y, x, p], wv.at[c, y, x, p], w1s.at[p, d - 1], w1r.at[p, d - 1], on_y(d) if p else on_x(d))

    def w_next(p, d):
        blk = wv.at[c, :, x, 1] if p else wv.at[c, y, :, 0]
        return remote(blk, blk, w2s.at[p, d - 1], w2r.at[p, d - 1], on_x(d) if p else on_y(d))

    def w_last(d):
        if d < 3:
            blk = wv.at[c, lax.rem(y + d + 1, 4)]
        elif d < 6:
            blk = wv.at[c, y, lax.rem(x + d - 2, 4)]
        else:
            blk = wv.at[c, y, x, c]
        return remote(blk, blk, w3s.at[d], w3r.at[d], sib)

    hops = [(p, d) for d in (1, 2, 3) for p in (0, 1)]
    w_pair.wait_recv()
    for p, d in hops:
        w_near(p, d).start()

    lens = diagonal(len_r[...].astype(F32), SEQ)
    gain_own = gain[:, pl.ds(pl.multiple_of(z * FB, 128), FB)].astype(F32)
    lane = iota((SEQ, 128), 1)
    sub = iota((SEQ, 128), 0)
    ends = jnp.sum(jnp.where(sub <= lane, lens, 0.0), axis=0, keepdims=True)
    starts = jnp.sum(jnp.where(sub < lane, lens, 0.0), axis=0, keepdims=True)
    for i, o in enumerate(OFFSETS):
        note(i, peer(o, 1), peer(o, -1), peer(o, 1)).wait_recv()
    mine[2].wait()
    place = meta_in[pl.ds(0, SEQ, 8), :]
    share = meta_in[pl.ds(4, SEQ, 8), :]
    place_r = jnp.where(iota((1, 128), 1) < SEQ, jnp.sum(jnp.where(sub == lane, place, 0.0), axis=0, keepdims=True), -1.0)
    share_r = jnp.sum(jnp.where(sub == lane, share, 0.0), axis=0, keepdims=True)
    column = iota((SEQ, SEQ * SLAB), 1) - iota((SEQ, SEQ * SLAB), 0) * SLAB
    here = (column >= 0) & (column < SLAB)
    key = jnp.sum(jnp.where(here, place[:, :1] * 128.0 + column.astype(F32), 0.0), axis=0, keepdims=True)

    def layout(b):
        at = pl.ds(b * TB, TB)
        i = (iota((TB, 128), 0) + b * TB).astype(F32)
        lane_f = iota((TB, 128), 1).astype(F32)
        hit = (i >= starts) & (i < ends)
        seg = jnp.sum(jnp.where(hit, lane_f, 0.0), axis=1, keepdims=True)
        pos = i - jnp.sum(jnp.where(hit, starts, 0.0), axis=1, keepdims=True)
        pos_b[at, :] = pos
        adv_b[at, :] = jnp.broadcast_to(
            jnp.sum(jnp.where(place_r == seg, share_r, 0.0), axis=1, keepdims=True), (TB, 128))
        rope[at, :] = lax.dot_general(
            jnp.where(pos == lane_f, 1.0, 0.0), table[...], (((1,), (0,)), ((), ())),
            precision=lax.Precision.HIGHEST, preferred_element_type=F32)
        pick[at, :] = jnp.where(seg * 128.0 + pos[:, :1] == key, 1.0, 0.0).astype(BF)

    for b in range(TOK // TB):
        layout(b)
    ring_c.hand_on()

    def pack(arr, lo, hi):
        def rows(b, carry):
            at = pl.ds(pl.multiple_of(b * 256, 256), 256)
            took = nn(pick[at, :], arr[...])
            packed[at, lo:hi] = took.astype(BF)
            xv[z, at, lo:hi] = (took * gain_own[:, lo:hi]).astype(BF)
            square = took * took
            lanes = sum(square[:, k:k + 128] for k in range(0, hi - lo, 128))
            sqc[at, :] = lanes if lo == 0 else sqc[at, :] + lanes
            return carry

        lax.fori_loop(0, TOK // 256, rows, 0)

    for i, o in enumerate(OFFSETS):
        part_a(i, peer(o, 1), peer(o, -1), peer(o, 1)).wait_recv()
    mine[0].wait()
    pack(arr_a, 0, FA)
    ring_a.start()
    ring_c.near()
    ring_c.end()
    cot_own.wait()
    keep = [pltpu.make_async_copy(cv, c_out, osem.at[0])]
    keep[0].start()
    ring_a.hand_on()
    for i, o in enumerate(OFFSETS):
        part_b(i, peer(o, 1), peer(o, -1), peer(o, 1)).wait_recv()
    mine[1].wait()
    for p, d in hops:
        w_near(p, d).wait_recv()
    for p, d in hops:
        w_next(p, d).start()
    pack(arr_b, FA, FB)
    ring_b.start()
    for b in range(TOK // TB):
        square = jnp.sum(sqc[b * TB:(b + 1) * TB, :], axis=1, keepdims=True)
        sq[:, b * TB:(b + 1) * TB] = jnp.transpose(jnp.broadcast_to(square, (TB, 128)))[:8, :]

    def tell(d):
        return remote(sq, sq_all.at[d - 1], qs.at[d], qr.at[d], {"tp": lax.rem(z + d, N_Z)})

    for d in (1, 2, 3):
        tell(d).start()
    kbuf[:TB, :] = jnp.zeros((TB, HD), BF)
    vbuf[:TB, :] = jnp.zeros((TB, HD), BF)
    dk[...] = jnp.zeros_like(dk)
    dv[...] = jnp.zeros_like(dv)
    ring_b.hand_on()
    ring_a.near()
    ring_a.end()
    for d in (1, 2, 3):
        tell(d).wait_recv()
    inv_t = lax.rsqrt((sq[...] + sq_all[0] + sq_all[1] + sq_all[2]) * (1.0 / D) + NORM_EPSILON)
    for b in range(TOK // TB):
        inv_b[b * TB:(b + 1) * TB, :] = jnp.transpose(jnp.broadcast_to(inv_t[:1, b * TB:(b + 1) * TB], (128, TB)))
    for p, d in hops:
        w_next(p, d).wait_recv()
    for d in range(7):
        w_last(d).start()
    for d in range(7):
        w_last(d).wait_recv()
    keep.append(pltpu.make_async_copy(wv, w_out, osem.at[1]))
    keep[1].start()

    def whole(h, blk):
        return wv[h, blk].reshape(FB, QC + KC)

    def project_c(d, carry):
        t = nn(cv[d], whole(1, d)[:, KC:])

        @pl.when(d == 0)
        def _():
            ga[...] = t

        @pl.when(d > 0)
        def _():
            ga[...] += t

        return carry

    lax.fori_loop(0, N_Z, project_c, 0)
    lin[...] = jnp.zeros_like(lin)

    def project_x(d, carry):
        blk = lax.rem(z + d, N_Z)
        lin[:, :QC + KC] += nn(xv[blk], whole(0, blk))
        lin[:, QC + KC:] += nn(xv[blk], whole(1, blk)[:, :KC])
        return carry

    project_x(0, 0)
    ring_b.near()
    lax.fori_loop(0, 2, lambda k, carry: project_x(1 + 2 * k, carry), 0)
    ring_b.end()
    keep.append(pltpu.make_async_copy(xv, x_out, osem.at[2]))
    keep[2].start()
    project_x(2, 0)

    def ready(b, carry):
        at = pl.ds(pl.multiple_of(b * TB, TB), TB)
        up = pl.ds(pl.multiple_of(b * TB + TB, TB), TB)
        inv = inv_b[at, :]
        cos, sin = rope[at, :HD], rope[at, HD:]
        for h in range(4):
            qrot[at, h * HD:(h + 1) * HD] = turn(lin[at, h * HD:(h + 1) * HD] * inv, cos, sin).astype(BF)
            gab[at, h * HD:(h + 1) * HD] = (ga[at, h * HD:(h + 1) * HD] * adv_b[at, :]).astype(BF)
        kbuf[up, :] = turn(lin[at, QC:QC + KC] * inv, cos, sin).astype(BF)
        vbuf[up, :] = (lin[at, QC + KC:] * inv).astype(BF)
        return carry

    lax.fori_loop(0, TOK // TB, ready, 0)
    scale = HD ** (-0.5)

    def attend(b, carry):
        at = pl.ds(pl.multiple_of(b * TB, TB), TB)
        win = pl.ds(pl.multiple_of(b * TB, TB), 2 * TB)
        q = stack(qrot[at, :])
        g = stack(gab[at, :])
        k, v = kbuf[win, :], vbuf[win, :]
        back = iota((TB, 2 * TB), 0) + TB - iota((TB, 2 * TB), 1)
        ok = (back >= 0) & (back.astype(F32) <= pos_b[at, :1])
        ok = jnp.concatenate([ok] * 4, axis=0)
        s = jnp.where(ok, nt(q, k) * scale, -1e30)
        e = jnp.where(ok, jnp.exp(s - jnp.max(s, axis=1, keepdims=True)), 0.0)
        p = e / jnp.sum(e, axis=1, keepdims=True)
        pb = p.astype(BF)
        o = unstack(nn(pb, v))
        dp = nt(g, v)
        ds = (p * (dp - jnp.sum(p * dp, axis=1, keepdims=True)) * scale).astype(BF)
        dq = nn(ds, k)
        dk[win, :] += tn(ds, q)
        dv[win, :] += tn(pb, g)
        prod = dq * q.astype(F32)
        mq[at, :] = prod[:TB] + prod[TB:2 * TB] + prod[2 * TB:3 * TB] + prod[3 * TB:]
        dq = unstack(dq)
        inv = inv_b[at, :]
        cos, sin = rope[at, :HD], rope[at, HD:]
        for h in range(4):
            col = slice(h * HD, (h + 1) * HD)
            grads[at, col] = (turn_back(dq[:, col], cos, sin) * inv).astype(BF)
            outs[at, col] = (o[:, col] * adv_b[at, :]).astype(BF)
        return carry

    lax.fori_loop(0, TOK // TB, attend, 0)

    def finish(b, carry):
        at = pl.ds(pl.multiple_of(b * TB, TB), TB)
        up = pl.ds(pl.multiple_of(b * TB + TB, TB), TB)
        inv = inv_b[at, :]
        cos, sin = rope[at, :HD], rope[at, HD:]
        gk, gv = dk[up, :], dv[up, :]
        grads[at, QC:QC + KC] = (turn_back(gk, cos, sin) * inv).astype(BF)
        grads[at, QC + KC:] = (gv * inv).astype(BF)
        m = mq[at, :] + gk * kbuf[up, :].astype(F32) + gv * vbuf[up, :].astype(F32)
        m = jnp.sum(m, axis=1, keepdims=True) * inv
        dots[:, at] = jnp.transpose(jnp.broadcast_to(m, (TB, 128)))[:8, :]
        return carry

    lax.fori_loop(0, TOK // TB, finish, 0)
    for ring in (ring_c, ring_a, ring_b):
        ring.sent()
    for kind in (note, part_a, part_b):
        for i, o in enumerate(OFFSETS):
            t = peer(o, 1)
            kind(i, t, me, t).wait_send()
    w_pair.wait_send()
    for p, d in hops:
        w_near(p, d).wait_send()
        w_next(p, d).wait_send()
    for d in range(7):
        w_last(d).wait_send()
    for d in (1, 2, 3):
        tell(d).wait_send()
    for k in keep:
        k.wait()


def grad_kernel(grads, outs, xf, cf, wf, dots, packed, gain, inv_b, adv_b, result, low_out, high_out,
                wv, wu, xv, cv, dots_all, sbuf, rbuf, dw, pair, r1, s1, r2, s2, fin,
                wsem, zs, zr, ds_, dr, ps, pr, s1s, s1r, s2s, s2r, fs, fr):
    z = lax.axis_index("tp")
    me = lax.axis_index("fsdp")
    y, x, c = me // 8, (me // 2) % 4, me % 2
    right, left, far = lax.rem(z + 1, N_Z), lax.rem(z + 3, N_Z), lax.rem(z + 2, N_Z)
    other = 1 - c
    sib = {"fsdp": y * 8 + x * 2 + other}

    def on_x(d):
        return {"fsdp": y * 8 + lax.rem(x + d, 4) * 2 + c}

    def on_y(d):
        return {"fsdp": lax.rem(y + d, 4) * 8 + x * 2 + c}

    order = [far, right, left, z]
    wl = [pltpu.make_async_copy(wf.at[0, t], wv.at[i], wsem.at[i, 0]) for i, t in enumerate(order)]
    ul = [pltpu.make_async_copy(wf.at[1, t, :, pl.ds(0, KC)], wu.at[i], wsem.at[i, 3]) for i, t in enumerate(order)]
    for k in wl + ul:
        k.start()
    rows = []
    for t in range(N_Z):
        rows += [pltpu.make_async_copy(xf.at[t], xv.at[t], wsem.at[t, 1]),
                 pltpu.make_async_copy(cf.at[t], cv.at[t], wsem.at[t, 2])]
    for k in rows:
        k.start()
    barrier = pltpu.get_barrier_semaphore()
    for d in (1, 2, 3):
        for who in ({"tp": lax.rem(z + d, N_Z)}, on_x(d), on_y(d)):
            pl.semaphore_signal(barrier, inc=1, device_id=who, device_id_type=MESH)
    pl.semaphore_signal(barrier, inc=1, device_id=sib, device_id_type=MESH)
    pl.semaphore_wait(barrier, 10)

    def note(d):
        return remote(dots, dots_all.at[d - 1], ds_.at[d], dr.at[d], {"tp": lax.rem(z + d, N_Z)})

    for d in (1, 2, 3):
        note(d).start()

    def ship(i):
        return remote(sbuf.at[i], rbuf.at[i], zs.at[i], zr.at[i], {"tp": right if i % 2 == 0 else left})

    def share(i, h):
        at = slice(h * HALF, (h + 1) * HALF)
        return nt(grads[at, :QC + KC], wv[i]) + nt(grads[at, QC + KC:], wu[i])

    def first(i, w, h):
        sbuf[i] = share(w, h).astype(BF)
        ship(i).start()

    wl[0].wait()
    ul[0].wait()
    first(0, 0, 0)
    first(1, 0, 1)
    for k in rows:
        k.wait()

    def swap(i):
        b = lax.rem(y + 1 + i, 4)
        return remote(dw.at[other, b], pair.at[b], ps.at[i], pr.at[i], sib)

    def terms(i, carry):
        b = lax.rem(y + 1 + i, 4)
        lo = tn(xv[b], grads[...]).astype(BF)
        hi = tn(cv[b], outs[...]).astype(BF)
        for j in range(8):
            at = slice(112 * j, 112 * (j + 1))
            dw[0, b, j // 2, j % 2] = lo[at, :QC + KC]
            dw[1, b, j // 2, j % 2, :, :KC] = lo[at, QC + KC:]
            dw[1, b, j // 2, j % 2, :, KC:] = hi[at]
        swap(i).start()
        return carry

    lax.fori_loop(0, 2, terms, 0)
    for k in (wl[1], ul[1], wl[2], ul[2]):
        k.wait()
    first(2, 1, 1)
    first(3, 2, 0)
    lax.fori_loop(2, 4, terms, 0)
    for i, w in ((4, 1), (5, 2)):
        a = share(w, i % 2)
        ship(i - 4).wait_recv()
        sbuf[i] = (a + rbuf[i - 4].astype(F32)).astype(BF)
        ship(i).start()

    def hop_y(d):
        return remote(dw.at[c, lax.rem(y + d, 4), :, 1], r1.at[1, d - 1], s1s.at[1, d - 1], s1r.at[1, d - 1], on_y(d))

    def hop_x(d):
        return remote(dw.at[c, :, lax.rem(x + d, 4), 0], r1.at[0, d - 1], s1s.at[0, d - 1], s1r.at[0, d - 1], on_x(d))

    def chip_sum(i, carry):
        b = lax.rem(y + 1 + i, 4)
        swap(i).wait_recv()
        for j in range(4):
            dw[c, b, j] = (dw[c, b, j].astype(F32) + pair[b, j].astype(F32)).astype(BF)

        @pl.when(i < 3)
        def _():
            hop_y(i + 1).start()

        return carry

    lax.fori_loop(0, 4, chip_sum, 0)
    for d in (1, 2, 3):
        hop_x(d).start()
    wl[3].wait()
    ul[3].wait()
    own = share(3, 0)
    sbuf[6] = own.astype(BF)
    own = share(3, 1)
    sbuf[7] = own.astype(BF)
    for d in (1, 2, 3):
        note(d).wait()
    m = (dots[...] + dots_all[0] + dots_all[1] + dots_all[2]) * (1.0 / D)

    for d in (1, 2, 3):
        hop_y(d).wait_recv()
        hop_x(d).wait_recv()
    for j in range(4):
        s1[1, j] = (dw[c, y, j, 1].astype(F32) + r1[1, 0, j].astype(F32) + r1[1, 1, j].astype(F32)
                    + r1[1, 2, j].astype(F32)).astype(BF)
        s1[0, j] = (dw[c, j, x, 0].astype(F32) + r1[0, 0, j].astype(F32) + r1[0, 1, j].astype(F32)
                    + r1[0, 2, j].astype(F32)).astype(BF)

    def last_x(d):
        return remote(s1.at[1, lax.rem(x + d, 4)], r2.at[1, d - 1], s2s.at[1, d - 1], s2r.at[1, d - 1], on_x(d))

    def last_y(d):
        return remote(s1.at[0, lax.rem(y + d, 4)], r2.at[0, d - 1], s2s.at[0, d - 1], s2r.at[0, d - 1], on_y(d))

    for d in (1, 2, 3):
        last_x(d).start()
        last_y(d).start()
    for d in (1, 2, 3):
        last_x(d).wait_recv()
        last_y(d).wait_recv()
    for p, own in ((0, s1[0, y]), (1, s1[1, x])):
        s2[p] = (own.astype(F32) + r2[p, 0].astype(F32) + r2[p, 1].astype(F32) + r2[p, 2].astype(F32)).astype(BF)
    trade = remote(s2.at[other], fin.at[c], fs.at[0], fr.at[0], sib)
    trade.start()
    for i in (2, 3, 4, 5):
        ship(i).wait_recv()
    gain_own = gain[:, pl.ds(pl.multiple_of(z * FB, 128), FB)].astype(F32)
    for b in range(TOK // TB):
        h, r = divmod(b * TB, HALF)
        at = slice(b * TB, (b + 1) * TB)
        hs = slice(r, r + TB)
        one, two = (4, 3) if h == 0 else (2, 5)
        s = sbuf[6 + h, hs, :].astype(F32) + rbuf[one, hs, :].astype(F32) + rbuf[two, hs, :].astype(F32)
        mc = jnp.transpose(jnp.broadcast_to(m[:1, at], (128, TB)))[:, :1]
        inv = inv_b[at, :1]
        result[at, :] = (adv_b[at, :1] * cv[z, at, :].astype(F32) + s * gain_own
                         - packed[at, :].astype(F32) * (inv * mc)).astype(BF)
    trade.wait()
    mine = s2[c]
    got = fin[other]
    low_out[...] = jnp.where(c == 0, mine, got)
    high_out[...] = jnp.where(c == 0, got, mine)
    for i in range(6):
        ship(i).wait_send()
    for i in range(4):
        swap(i).wait_send()
    for d in (1, 2, 3):
        hop_x(d).wait_send()
        hop_y(d).wait_send()
        last_x(d).wait_send()
        last_y(d).wait_send()


def split_kernel(result, low, high, res, res_q, res_k, res_v, res_o):
    res[...] = result[...]
    res_q[...] = low[:, :QC]
    res_k[...] = low[:, QC:]
    res_v[...] = high[:, :KC]
    res_o[...] = high[:, KC:]


def sds(shape, dtype=BF):
    return jax.ShapeDtypeStruct(shape, dtype)


def params(**kw):
    return pltpu.CompilerParams(vmem_limit_bytes=LIMIT, has_side_effects=True, **kw)


def rope_table():
    i = np.arange(HD // 2, dtype=np.float32)
    frequency = np.float32(ROPE_BASE) ** (-(np.float32(2.0) * i) / np.float32(HD))
    angle = np.arange(128, dtype=np.float32)[:, None] * frequency[None, :]
    c, s = np.cos(angle), np.sin(angle)
    return np.concatenate([c, c, -s, s], axis=1).astype(np.float32)


def per_device(roll_rows, dest, lengths, clusters, log_prob_grad, gain, w_q, w_k, w_v, w_o_t):
    gain = gain.reshape(1, D)
    send_a, send_b, meta = pl.pallas_call(
        stage_kernel, out_shape=(sds((SEQ * SLAB, FA)), sds((SEQ * SLAB, FB - FA)), sds((SEQ * 8, 128), F32)),
        in_specs=[SMEM, VMEM, VMEM, VMEM], out_specs=(VMEM,) * 3, compiler_params=params(),
    )(dest, dest.reshape(1, SEQ), clusters.reshape(1, SEQ), roll_rows)
    n_o = len(OFFSETS)
    width = QC + 2 * KC
    half = (112, QC + KC)
    v = pltpu.VMEM
    ring = [DMA((6,)), DMA((6,))]
    rows, cot, weights, packed, grads, outs, inv_b, adv_b, dots = pl.pallas_call(
        front_kernel,
        out_shape=(sds((N_Z, TOK, FB)), sds((N_Z, TOK, FB)), sds((2, 4, 4, 2) + half), sds((TOK, FB)),
                   sds((TOK, width)), sds((TOK, QC)), sds((TOK, 128), F32), sds((TOK, 128), F32), sds((8, TOK), F32)),
        in_specs=[HBM] * 4 + [VMEM] * 7, out_specs=(HBM,) * 3 + (VMEM,) * 6,
        scratch_shapes=[
            v((SEQ * SLAB, FA), BF), v((SEQ * SLAB, FB - FA), BF), v((SEQ * 8, 128), F32), v((TOK, SEQ * SLAB), BF),
            v((N_Z, TOK, FB), BF), v((N_Z, TOK, FB), BF), v((2,) + half, BF), v((2, 4, 4, 2) + half, BF),
            v((8, TOK), F32), v((3, 8, TOK), F32), v((TOK, 128), F32), v((TOK, 2 * HD), F32), v((TOK, 128), F32),
            v((TOK, width), F32), v((TOK, QC), F32),
            v((TOK, QC), BF), v((TOK + TB, HD), BF), v((TOK + TB, HD), BF),
            v((TOK, QC), BF), v((TOK + TB, HD), F32), v((TOK + TB, HD), F32), v((TOK, HD), F32),
            DMA((4,)), DMA((3,))] + [DMA((n_o,))] * 6 + ring * 3 + [DMA((4,)), DMA((4,)), DMA((1,)), DMA((1,))]
        + [DMA((2, 3))] * 4 + [DMA((7,))] * 2,
        compiler_params=params(collective_id=0),
    )(send_a, send_b, meta, log_prob_grad, lengths, gain, jnp.asarray(rope_table()), w_q, w_k, w_v, w_o_t)
    result, low, high = pl.pallas_call(
        grad_kernel,
        out_shape=(sds((TOK, FB)), sds(half), sds(half)),
        in_specs=[VMEM, VMEM] + [HBM] * 3 + [VMEM] * 5, out_specs=(VMEM,) * 3,
        scratch_shapes=[
            v((N_Z, FB, QC + KC), BF), v((N_Z, FB, KC), BF), v((N_Z, TOK, FB), BF), v((N_Z, TOK, FB), BF),
            v((3, 8, TOK), F32), v((8, HALF, FB), BF), v((6, HALF, FB), BF),
            v((2, 4, 4, 2) + half, BF), v((4, 4, 2) + half, BF),
            v((2, 3, 4) + half, BF), v((2, 4) + half, BF), v((2, 3) + half, BF),
            v((2,) + half, BF), v((2,) + half, BF),
            DMA((N_Z, 4)), DMA((6,)), DMA((6,)), DMA((4,)), DMA((4,)), DMA((4,)), DMA((4,)),
            DMA((2, 3)), DMA((2, 3)), DMA((2, 3)), DMA((2, 3)), DMA((1,)), DMA((1,))],
        compiler_params=params(collective_id=1),
    )(grads, outs, rows, cot, weights.reshape(2, N_Z, FB, QC + KC), dots, packed, gain, inv_b, adv_b)
    return pl.pallas_call(
        split_kernel,
        out_shape=(sds((TOK, FB)), sds((112, QC)), sds((112, KC)), sds((112, KC)), sds((112, QC))),
        in_specs=[VMEM] * 3, out_specs=(VMEM,) * 5, compiler_params=params(),
    )(result, low, high)


def solution(mesh):
    in_specs = (
        P("fsdp", None, "tp"), P("fsdp"), P("fsdp", None), P("fsdp"), P("fsdp", "tp"), P(),
        P("fsdp", "tp"), P("fsdp", "tp"), P("fsdp", "tp"), P("fsdp", "tp"),
    )
    out_specs = (P("fsdp", "tp"),) * 5
    return jax.shard_map(per_device, mesh=mesh, in_specs=in_specs, out_specs=out_specs, check_vma=False)
```

time: 251 us -> 205 us (0.82)
  Pallas kernels: 225 us -> 202 us
  between operations: 14.1 us -> 0.65 us
  local copies, waits for them, and re-layouts: 9.65 us -> 1.31 us
    pallas_call x6 -> x4, Pallas kernels: 225 us -> 202 us  [the longest x1 128 us: per_device(): pl.pallas_call(front_kernel, out_shape=(sds((N_Z, TOK, FB)), sds((N_Z, TO...]
    unnamed x5 -> x0, local copies, waits for them, and re-layouts: 8.34 us -> none
  transfers between devices with their start and end apart: 1 -> 0, of which waited for: 0 -> 0; matrix products, arithmetic and copies ran while one was open for 1% -> 0% of each run, Pallas kernels for 53% -> 0%
where the time goes in v3:
time: 205 us; the launch traced here: 204 us
  Pallas kernels  202 us (99%)
    pallas_call x1, Pallas kernels, per_device(): pl.pallas_call(front_kernel, out_shape=(sds((N_Z, TOK, FB)), sds((N_Z, TO...  128 us
    pallas_call x1, Pallas kernels, per_device(): pl.pallas_call(grad_kernel, out_shape=(sds((TOK, FB)), sds(half), sds(hal...  66.6 us
    pallas_call x1, Pallas kernels, per_device(): pl.pallas_call(stage_kernel, out_shape=(sds((SEQ * SLAB, FA)), sds((SEQ *...  5.12 us

profile of v3, /device:TPU:1, one launch (start us, length us, event | category | flops | bytes accessed | tf_op | source)
XLA Modules:
  0.0 204.4 jit_solution(17978742902172733735)
XLA Ops:
  0.6 1.3 reshape.24.gain
  1.9 5.1 %shard_map.146 = (bf16[2560,512]{1,0:T(8,128)(2,1)}, bf16[2560,384]{1,0:T(8,128)(2,1)}, f32[256,128]{1,0:T(8,128)}) custom-call(s32[32]{0:T(128)} %dest_s.1, s32[1,32]{1,0:T(1,128)} %bitcast.4, s32[1,32]{1,0:T(1,128)} %bitcast.5, bf16[32,72,896]{2,1,0:T(8,128)(2,1)} %roll.1), custom_call_target="tpu_custom_call" | custom-call | tf_op jit(solution)/shard_map/pallas_call | solution.py:639
  7.1 128.1 %shard_map.147 = (bf16[4,768,896]{2,1,0:T(8,128)(2,1)}, bf16[4,768,896]{2,1,0:T(8,128)(2,1)}, bf16[2,4,4,2,112,640]{5,4,3,2,1,0:T(8,128)(2,1)}, bf16[768,896]{1,...) custom-call(bf16[2560,512]{1,0:T(8,128)(2,1)} %get-tuple-element.20., ...), custom_call_target="tpu_custom_call" | custom-call | tf_op jit(solution)/shard_map/pallas_call | solution.py:648
  135.2 66.6 %shard_map.148 = (bf16[768,896]{1,0:T(8,128)(2,1)}, bf16[112,640]{1,0:T(8,128)(2,1)}, bf16[112,640]{1,0:T(8,128)(2,1)}) custom-call(bf16[768,768]{1,0:T(8,128)(2,1)} %get-tuple-element.23.grads, bf16[768,512]{1,0:T(8,128)(2,1)} %get-tuple-element.24.outs, bf16[4,768,896]{2,1,0:T(8,128)(2,1)} %get-tuple-element.25.xf, ...), custom_call_target="tpu_custom_call" | custom-call | tf_op jit(solution)/shard_map/pallas_call | solution.py:664
  201.8 2.7 %shard_map.149 = (bf16[768,896]{1,0:T(8,128)(2,1)}, bf16[112,512]{1,0:T(8,128)(2,1)}, bf16[112,128]{1,0:T(8,128)(2,1)}, bf16[112,128]{1,0:T(8,128)(2,1)}, bf16[112,512]{1,0:T(8,128)(2,1)}) custom-call(bf16[768,896]{1,0:T(8,128)(2,1)} %get-tuple-element.32.result, bf16[112,640]{1,0:T(8,128)(2,1)} %get-tuple-element.33.low, ...), custom_call_target="tpu_custom_call" | custom-call | tf_op jit(solution)/shard_map/pallas_call | solution.py:678

commit v4 on v3

v4 whole, which is shorter than its diff:
```python
import jax
import jax.numpy as jnp
import numpy as np
from jax import lax
from jax.experimental import pallas as pl
from jax.experimental.pallas import tpu as pltpu
from jax.sharding import PartitionSpec as P

HD = 128
GSIZE = 16
ROPE_BASE = 1000000.0
NORM_EPSILON = 1e-06
MESH = pl.DeviceIdType.MESH
BF = jnp.bfloat16
F32 = jnp.float32
HBM = pl.BlockSpec(memory_space=pl.ANY)
VMEM = pl.BlockSpec(memory_space=pltpu.VMEM)
SMEM = pl.BlockSpec(memory_space=pltpu.SMEM)
DMA = pltpu.SemaphoreType.DMA
LIMIT = 60 * 2**20

N_F = 32
N_Z = 4
SEQ = 32
MAXLEN = 72
TOK = 768
HALF = TOK // 2
FB = 896
FA = 512
SLAB = 80
D = 3584
QC = 512
KC = 128
TB = 128

CHIPS = [(0, 1), (1, 0), (0, 3), (3, 0), (1, 1), (3, 3), (1, 3), (3, 1),
         (0, 2), (2, 0), (1, 2), (2, 1), (3, 2), (2, 3), (2, 2)]
OFFSETS = [(0, 0, 1)] + [(a, b, c) for c in range(2) for a, b in CHIPS]


def nt(a, b):
    return lax.dot_general(a, b, (((1,), (1,)), ((), ())), preferred_element_type=F32)


def tn(a, b):
    return lax.dot_general(a, b, (((0,), (0,)), ((), ())), preferred_element_type=F32)


def nn(a, b):
    return lax.dot_general(a, b, (((1,), (0,)), ((), ())), preferred_element_type=F32)


def iota(shape, dim):
    return lax.broadcasted_iota(jnp.int32, shape, dim)


def diagonal(row, n):
    return jnp.sum(jnp.where(iota((n, n), 0) == iota((n, n), 1), row, 0.0), axis=1, keepdims=True)


def stage_kernel(dest_s, dest_r, clus_r, roll, send_a, send_b, meta):
    def place(s, c):
        at = pl.ds(pl.multiple_of((dest_s[s] // SEQ) * SLAB, 16), SLAB)
        v = jnp.concatenate([roll[s], jnp.zeros((SLAB - MAXLEN, FB), BF)], axis=0)
        send_a[at, :] = v[:, :FA]
        send_b[at, :] = v[:, FA:]
        return c

    lax.fori_loop(0, SEQ, place, 0)
    clus = clus_r[...].astype(F32)
    group = iota((SEQ, SEQ), 0) // GSIZE == iota((SEQ, SEQ), 1) // GSIZE
    same = jnp.where((diagonal(clus, SEQ) == clus) & group, 1.0 / GSIZE, 0.0)
    share_c = jnp.sum(same, axis=1, keepdims=True)
    share_r = jnp.sum(same, axis=0, keepdims=True)
    mean_r = jnp.sum(jnp.where(group, share_c, 0.0), axis=0, keepdims=True) * (1.0 / GSIZE)
    adv_r = (share_r - mean_r).astype(BF).astype(F32)
    rows = iota((SEQ * 8, SEQ), 0)
    dest_v = dest_r[...]
    hit = dest_v // SEQ == rows // 8
    what = jnp.where(rows % 8 < 4, (dest_v % SEQ).astype(F32), adv_r)
    meta[...] = jnp.broadcast_to(jnp.sum(jnp.where(hit, what, 0.0), axis=1, keepdims=True), (SEQ * 8, 128))


def remote(src, dst, ss, rs, who):
    return pltpu.make_async_remote_copy(
        src_ref=src, dst_ref=dst, send_sem=ss, recv_sem=rs, device_id=who, device_id_type=MESH)


class Ring:
    def __init__(self, own, dst, cols, z, ss, rs):
        self.own, self.dst, self.cols, self.z, self.ss, self.rs = own, dst, cols, z, ss, rs
        self.right, self.left, self.far = (lax.rem(z + d, N_Z) for d in (1, 3, 2))

    def copy(self, i, blk, src=None):
        half = (0, 1, 1, 0, 0, 1)[i]
        at = pl.ds(half * HALF, HALF)
        to = self.right if i % 2 == 0 else self.left
        src = self.own if src is None else src
        return remote(src.at[at, self.cols], self.dst.at[blk, at, self.cols], self.ss.at[i], self.rs.at[i], {"tp": to})

    def start(self):
        for i in range(4):
            self.copy(i, self.z).start()

    def hand_on(self):
        for i, blk in ((0, self.left), (1, self.right)):
            self.copy(i, blk).wait_recv()
            self.copy(i + 4, blk, self.dst.at[blk]).start()

    def near(self):
        self.copy(2, self.left).wait_recv()
        self.copy(3, self.right).wait_recv()

    def end(self):
        self.copy(4, self.far).wait_recv()
        self.copy(5, self.far).wait_recv()

    def sent(self):
        for i in range(4):
            self.copy(i, self.z).wait_send()
        self.copy(4, self.left, self.dst.at[self.left]).wait_send()
        self.copy(5, self.right, self.dst.at[self.right]).wait_send()


def unstack(v):
    return jnp.concatenate([v[h * TB:(h + 1) * TB] for h in range(4)], axis=1)


def stack(v):
    return jnp.concatenate([v[:, h * HD:(h + 1) * HD] for h in range(4)], axis=0)


def turn(v, cos, sin):
    return v * cos + jnp.concatenate([v[:, HD // 2:], v[:, :HD // 2]], axis=1) * sin


def turn_back(v, cos, sin):
    return v * cos - jnp.concatenate([v[:, HD // 2:], v[:, :HD // 2]], axis=1) * sin


def whole_kernel(send_a, send_b, meta, cot, len_r, gain, table, w_q, w_k, w_v, w_o,
                 result, low_out, high_out,
                 arr, meta_in, xv, cv, wsh, wv, sq, sq_all, sqc, rope, pos_b, grads, outs, inv_b, adv_b, dots,
                 dots_all, rbuf, pair, r1, r2, s2, fin,
                 lsem, as_, ar, bs, br, ms, mr, zs, zr, us, ur, vs, vr, qs, qr,
                 w0s, w0r, w1s, w1r, w2s, w2r, w3s, w3r,
                 gs, gr, ds_, dr, ps, pr, s1s, s1r, s2s, s2r, fs, fr):
    packed = result
    me = lax.axis_index("fsdp")
    z = lax.axis_index("tp")
    y, x, c = me // 8, (me // 2) % 4, me % 2
    other = 1 - c
    sib = {"fsdp": y * 8 + x * 2 + other}

    def peer(o, s):
        return lax.rem(y + s * o[0] + 4, 4) * 8 + lax.rem(x + s * o[1] + 4, 4) * 2 + lax.rem(c + s * o[2] + 2, 2)

    def on_x(d):
        return {"fsdp": peer((0, d, 0), 1)}

    def on_y(d):
        return {"fsdp": peer((d, 0, 0), 1)}

    cot_own = pltpu.make_async_copy(cot, cv.at[z], lsem.at[0])
    cot_own.start()
    barrier = pltpu.get_barrier_semaphore()
    for o in OFFSETS:
        pl.semaphore_signal(barrier, inc=1, device_id={"fsdp": peer(o, 1)}, device_id_type=MESH)
    for d in (1, 2, 3):
        pl.semaphore_signal(barrier, inc=1, device_id={"tp": lax.rem(z + d, N_Z)}, device_id_type=MESH)
    pl.semaphore_wait(barrier, len(OFFSETS) + 3)

    ring_c = Ring(cot, cv, pl.ds(0, FB), z, zs, zr)
    ring_a = Ring(xv.at[z], xv, pl.ds(0, FA), z, us, ur)
    ring_b = Ring(xv.at[z], xv, pl.ds(FA, FB - FA), z, vs, vr)
    ring_c.start()

    def slab(k):
        return pl.ds(pl.multiple_of(k * SLAB, 16), SLAB)

    def eight(k):
        return pl.ds(pl.multiple_of(k * 8, 8), 8)

    def part_a(i, frm, to, who):
        return remote(send_a.at[slab(frm)], arr.at[slab(to), pl.ds(0, FA)], as_.at[i], ar.at[i], {"fsdp": who})

    def part_b(i, frm, to, who):
        return remote(send_b.at[slab(frm)], arr.at[slab(to), pl.ds(FA, FB - FA)], bs.at[i], br.at[i], {"fsdp": who})

    def note(i, frm, to, who):
        return remote(meta.at[eight(frm)], meta_in.at[eight(to)], ms.at[i], mr.at[i], {"fsdp": who})

    for kind in (note, part_a, part_b):
        for i, o in enumerate(OFFSETS):
            t = peer(o, 1)
            kind(i, t, me, t).start()
    mine = [pltpu.make_async_copy(send_a.at[slab(me)], arr.at[slab(me), pl.ds(0, FA)], lsem.at[1]),
            pltpu.make_async_copy(send_b.at[slab(me)], arr.at[slab(me), pl.ds(FA, FB - FA)], lsem.at[2]),
            pltpu.make_async_copy(meta.at[eight(me)], meta_in.at[eight(me)], lsem.at[3])]
    for k in mine:
        k.start()

    wsh[0, :, :QC] = w_q[...]
    wsh[0, :, QC:] = w_k[...]
    wsh[1, :, :KC] = w_v[...]
    wsh[1, :, KC:] = w_o[...]
    wv[0, y, x, c] = wsh[0]
    wv[1, y, x, c] = wsh[1]
    w_pair = remote(wsh.at[other], wv.at[other, y, x, c], w0s.at[0], w0r.at[0], sib)
    w_pair.start()

    def w_near(p, d):
        return remote(wv.at[c, y, x, p], wv.at[c, y, x, p], w1s.at[p, d - 1], w1r.at[p, d - 1], on_y(d) if p else on_x(d))

    def w_next(p, d):
        blk = wv.at[c, :, x, 1] if p else wv.at[c, y, :, 0]
        return remote(blk, blk, w2s.at[p, d - 1], w2r.at[p, d - 1], on_x(d) if p else on_y(d))

    def w_last(d):
        if d < 3:
            blk = wv.at[c, lax.rem(y + d + 1, 4)]
        elif d < 6:
            blk = wv.at[c, y, lax.rem(x + d - 2, 4)]
        else:
            blk = wv.at[c, y, x, c]
        return remote(blk, blk, w3s.at[d], w3r.at[d], sib)

    hops = [(p, d) for d in (1, 2, 3) for p in (0, 1)]
    w_pair.wait_recv()
    for p, d in hops:
        w_near(p, d).start()

    lens = diagonal(len_r[...].astype(F32), SEQ)
    gain_own = gain[:, pl.ds(pl.multiple_of(z * FB, 128), FB)].astype(F32)
    lane = iota((SEQ, 128), 1)
    sub = iota((SEQ, 128), 0)
    ends = jnp.sum(jnp.where(sub <= lane, lens, 0.0), axis=0, keepdims=True)
    starts = jnp.sum(jnp.where(sub < lane, lens, 0.0), axis=0, keepdims=True)
    for i, o in enumerate(OFFSETS):
        note(i, peer(o, 1), peer(o, -1), peer(o, 1)).wait_recv()
    mine[2].wait()
    place = meta_in[pl.ds(0, SEQ, 8), :]
    share = meta_in[pl.ds(4, SEQ, 8), :]
    place_r = jnp.where(iota((1, 128), 1) < SEQ, jnp.sum(jnp.where(sub == lane, place, 0.0), axis=0, keepdims=True), -1.0)
    share_r = jnp.sum(jnp.where(sub == lane, share, 0.0), axis=0, keepdims=True)
    column = iota((SEQ, SEQ * SLAB), 1) - iota((SEQ, SEQ * SLAB), 0) * SLAB
    here = (column >= 0) & (column < SLAB)
    key = jnp.sum(jnp.where(here, place[:, :1] * 128.0 + column.astype(F32), 0.0), axis=0, keepdims=True)

    def packing(pick):
        def layout(b):
            at = pl.ds(b * TB, TB)
            i = (iota((TB, 128), 0) + b * TB).astype(F32)
            lane_f = iota((TB, 128), 1).astype(F32)
            hit = (i >= starts) & (i < ends)
            seg = jnp.sum(jnp.where(hit, lane_f, 0.0), axis=1, keepdims=True)
            pos = i - jnp.sum(jnp.where(hit, starts, 0.0), axis=1, keepdims=True)
            pos_b[at, :] = pos
            adv_b[at, :] = jnp.broadcast_to(
                jnp.sum(jnp.where(place_r == seg, share_r, 0.0), axis=1, keepdims=True), (TB, 128))
            rope[at, :] = lax.dot_general(
                jnp.where(pos == lane_f, 1.0, 0.0), table[...], (((1,), (0,)), ((), ())),
                precision=lax.Precision.HIGHEST, preferred_element_type=F32)
            pick[at, :] = jnp.where(seg * 128.0 + pos[:, :1] == key, 1.0, 0.0).astype(BF)

        for b in range(TOK // TB):
            layout(b)
        ring_c.hand_on()

        def pack(lo, hi):
            def rows(b, carry):
                at = pl.ds(pl.multiple_of(b * 256, 256), 256)
                took = nn(pick[at, :], arr[:, lo:hi])
                packed[at, lo:hi] = took.astype(BF)
                xv[z, at, lo:hi] = (took * gain_own[:, lo:hi]).astype(BF)
                square = took * took
                lanes = sum(square[:, k:k + 128] for k in range(0, hi - lo, 128))
                sqc[at, :] = lanes if lo == 0 else sqc[at, :] + lanes
                return carry

            lax.fori_loop(0, TOK // 256, rows, 0)

        for i, o in enumerate(OFFSETS):
            part_a(i, peer(o, 1), peer(o, -1), peer(o, 1)).wait_recv()
        mine[0].wait()
        pack(0, FA)
        ring_a.start()
        ring_c.near()
        ring_c.end()
        cot_own.wait()
        ring_a.hand_on()
        for i, o in enumerate(OFFSETS):
            part_b(i, peer(o, 1), peer(o, -1), peer(o, 1)).wait_recv()
        mine[1].wait()
        for p, d in hops:
            w_near(p, d).wait_recv()
        for p, d in hops:
            w_next(p, d).start()
        pack(FA, FB)
        ring_b.start()
    pl.run_scoped(packing, scratch((TOK, SEQ * SLAB)))
    for b in range(TOK // TB):
        square = jnp.sum(sqc[b * TB:(b + 1) * TB, :], axis=1, keepdims=True)
        sq[:, b * TB:(b + 1) * TB] = jnp.transpose(jnp.broadcast_to(square, (TB, 128)))[:8, :]

    def tell(d):
        return remote(sq, sq_all.at[d - 1], qs.at[d], qr.at[d], {"tp": lax.rem(z + d, N_Z)})

    for d in (1, 2, 3):
        tell(d).start()
    ring_b.hand_on()
    ring_a.near()
    ring_a.end()
    for d in (1, 2, 3):
        tell(d).wait_recv()
    inv_t = lax.rsqrt((sq[...] + sq_all[0] + sq_all[1] + sq_all[2]) * (1.0 / D) + NORM_EPSILON)
    for b in range(TOK // TB):
        inv_b[b * TB:(b + 1) * TB, :] = jnp.transpose(jnp.broadcast_to(inv_t[:1, b * TB:(b + 1) * TB], (128, TB)))
    for p, d in hops:
        w_next(p, d).wait_recv()
    for d in range(7):
        w_last(d).start()
    for d in range(7):
        w_last(d).wait_recv()

    def whole(h, blk):
        return wv[h, blk].reshape(FB, QC + KC)

    def attention(kbuf, vbuf, dk, dv, lin, ga, qrot, gab, mq):
        kbuf[:TB, :] = jnp.zeros((TB, HD), BF)
        vbuf[:TB, :] = jnp.zeros((TB, HD), BF)
        dk[...] = jnp.zeros_like(dk)
        dv[...] = jnp.zeros_like(dv)
        def project_c(d, carry):
            t = nn(cv[d], whole(1, d)[:, KC:])

            @pl.when(d == 0)
            def _():
                ga[...] = t

            @pl.when(d > 0)
            def _():
                ga[...] += t

            return carry

        lax.fori_loop(0, N_Z, project_c, 0)
        lin[...] = jnp.zeros_like(lin)

        def project_x(d, carry):
            blk = lax.rem(z + d, N_Z)
            lin[:, :QC + KC] += nn(xv[blk], whole(0, blk))
            lin[:, QC + KC:] += nn(xv[blk], whole(1, blk)[:, :KC])
            return carry

        project_x(0, 0)
        ring_b.near()
        lax.fori_loop(0, 2, lambda k, carry: project_x(1 + 2 * k, carry), 0)
        ring_b.end()
        project_x(2, 0)

        def ready(b, carry):
            at = pl.ds(pl.multiple_of(b * TB, TB), TB)
            up = pl.ds(pl.multiple_of(b * TB + TB, TB), TB)
            inv = inv_b[at, :]
            cos, sin = rope[at, :HD], rope[at, HD:]
            for h in range(4):
                qrot[at, h * HD:(h + 1) * HD] = turn(lin[at, h * HD:(h + 1) * HD] * inv, cos, sin).astype(BF)
                gab[at, h * HD:(h + 1) * HD] = (ga[at, h * HD:(h + 1) * HD] * adv_b[at, :]).astype(BF)
            kbuf[up, :] = turn(lin[at, QC:QC + KC] * inv, cos, sin).astype(BF)
            vbuf[up, :] = (lin[at, QC + KC:] * inv).astype(BF)
            return carry

        lax.fori_loop(0, TOK // TB, ready, 0)
        scale = HD ** (-0.5)

        def attend(b, carry):
            at = pl.ds(pl.multiple_of(b * TB, TB), TB)
            win = pl.ds(pl.multiple_of(b * TB, TB), 2 * TB)
            q = stack(qrot[at, :])
            g = stack(gab[at, :])
            k, v = kbuf[win, :], vbuf[win, :]
            back = iota((TB, 2 * TB), 0) + TB - iota((TB, 2 * TB), 1)
            ok = (back >= 0) & (back.astype(F32) <= pos_b[at, :1])
            ok = jnp.concatenate([ok] * 4, axis=0)
            s = jnp.where(ok, nt(q, k) * scale, -1e30)
            e = jnp.where(ok, jnp.exp(s - jnp.max(s, axis=1, keepdims=True)), 0.0)
            p = e / jnp.sum(e, axis=1, keepdims=True)
            pb = p.astype(BF)
            o = unstack(nn(pb, v))
            dp = nt(g, v)
            ds = (p * (dp - jnp.sum(p * dp, axis=1, keepdims=True)) * scale).astype(BF)
            dq = nn(ds, k)
            dk[win, :] += tn(ds, q)
            dv[win, :] += tn(pb, g)
            prod = dq * q.astype(F32)
            mq[at, :] = prod[:TB] + prod[TB:2 * TB] + prod[2 * TB:3 * TB] + prod[3 * TB:]
            dq = unstack(dq)
            inv = inv_b[at, :]
            cos, sin = rope[at, :HD], rope[at, HD:]
            for h in range(4):
                col = slice(h * HD, (h + 1) * HD)
                grads[at, col] = (turn_back(dq[:, col], cos, sin) * inv).astype(BF)
                outs[at, col] = (o[:, col] * adv_b[at, :]).astype(BF)
            return carry

        lax.fori_loop(0, TOK // TB, attend, 0)

        def finish(b, carry):
            at = pl.ds(pl.multiple_of(b * TB, TB), TB)
            up = pl.ds(pl.multiple_of(b * TB + TB, TB), TB)
            inv = inv_b[at, :]
            cos, sin = rope[at, :HD], rope[at, HD:]
            gk, gv = dk[up, :], dv[up, :]
            grads[at, QC:QC + KC] = (turn_back(gk, cos, sin) * inv).astype(BF)
            grads[at, QC + KC:] = (gv * inv).astype(BF)
            m = mq[at, :] + gk * kbuf[up, :].astype(F32) + gv * vbuf[up, :].astype(F32)
            m = jnp.sum(m, axis=1, keepdims=True) * inv
            dots[:, at] = jnp.transpose(jnp.broadcast_to(m, (TB, 128)))[:8, :]
            return carry

        lax.fori_loop(0, TOK // TB, finish, 0)
    v = scratch
    pl.run_scoped(attention, v((TOK + TB, HD)), v((TOK + TB, HD)), v((TOK + TB, HD), F32), v((TOK + TB, HD), F32),
                  v((TOK, WIDTH), F32), v((TOK, QC), F32), v((TOK, QC)), v((TOK, QC)), v((TOK, HD), F32))
    ring_c.sent()
    right, left, far = lax.rem(z + 1, N_Z), lax.rem(z + 3, N_Z), lax.rem(z + 2, N_Z)
    order = [far, right, left, z]

    def gradients(dw, s1):
        def dot_note(d):
            return remote(dots, dots_all.at[d - 1], ds_.at[d], dr.at[d], {"tp": lax.rem(z + d, N_Z)})

        for d in (1, 2, 3):
            dot_note(d).start()

        def ship(i):
            return remote(arr.at[pl.ds(i * HALF, HALF)], rbuf.at[i], gs.at[i], gr.at[i], {"tp": right if i % 2 == 0 else left})

        def share(i, h):
            at = slice(h * HALF, (h + 1) * HALF)
            return nt(grads[at, :QC + KC], whole(0, order[i])) + nt(grads[at, QC + KC:], whole(1, order[i])[:, :KC])

        def first(i, w, h):
            arr[i * HALF:(i + 1) * HALF, :] = share(w, h).astype(BF)
            ship(i).start()

        first(0, 0, 0)
        first(1, 0, 1)
        def swap(i):
            b = lax.rem(y + 1 + i, 4)
            return remote(dw.at[other, b], pair.at[b], ps.at[i], pr.at[i], sib)

        def terms(i, carry):
            b = lax.rem(y + 1 + i, 4)
            def place(h, cols, v):
                for j in range(8):
                    dw[h, b, j // 2, j % 2, :, cols] = v[112 * j:112 * (j + 1)]

            place(0, slice(0, QC), tn(xv[b], grads[:, :QC]).astype(BF))
            t = tn(xv[b], grads[:, QC:]).astype(BF)
            place(0, slice(QC, QC + KC), t[:, :KC])
            place(1, slice(0, KC), t[:, KC:])
            place(1, slice(KC, QC + KC), tn(cv[b], outs[...]).astype(BF))
            swap(i).start()
            return carry

        lax.fori_loop(0, 2, terms, 0)
        first(2, 1, 1)
        first(3, 2, 0)
        lax.fori_loop(2, 4, terms, 0)
        for i, w in ((4, 1), (5, 2)):
            a = share(w, i % 2)
            ship(i - 4).wait_recv()
            arr[i * HALF:(i + 1) * HALF, :] = (a + rbuf[i - 4].astype(F32)).astype(BF)
            ship(i).start()

        def hop_y(d):
            return remote(dw.at[c, lax.rem(y + d, 4), :, 1], r1.at[1, d - 1], s1s.at[1, d - 1], s1r.at[1, d - 1], on_y(d))

        def hop_x(d):
            return remote(dw.at[c, :, lax.rem(x + d, 4), 0], r1.at[0, d - 1], s1s.at[0, d - 1], s1r.at[0, d - 1], on_x(d))

        def chip_sum(i, carry):
            b = lax.rem(y + 1 + i, 4)
            swap(i).wait_recv()
            for j in range(4):
                dw[c, b, j] = (dw[c, b, j].astype(F32) + pair[b, j].astype(F32)).astype(BF)

            @pl.when(i < 3)
            def _():
                hop_y(i + 1).start()

            return carry

        lax.fori_loop(0, 4, chip_sum, 0)
        for d in (1, 2, 3):
            hop_x(d).start()
        for h in range(2):
            cv[right, h * HALF:(h + 1) * HALF, :] = share(3, h).astype(BF)
        for d in (1, 2, 3):
            dot_note(d).wait()
        m = (dots[...] + dots_all[0] + dots_all[1] + dots_all[2]) * (1.0 / D)

        for d in (1, 2, 3):
            hop_y(d).wait_recv()
            hop_x(d).wait_recv()
        for j in range(4):
            s1[1, j] = (dw[c, y, j, 1].astype(F32) + r1[1, 0, j].astype(F32) + r1[1, 1, j].astype(F32)
                        + r1[1, 2, j].astype(F32)).astype(BF)
            s1[0, j] = (dw[c, j, x, 0].astype(F32) + r1[0, 0, j].astype(F32) + r1[0, 1, j].astype(F32)
                        + r1[0, 2, j].astype(F32)).astype(BF)

        def last_x(d):
            return remote(s1.at[1, lax.rem(x + d, 4)], r2.at[1, d - 1], s2s.at[1, d - 1], s2r.at[1, d - 1], on_x(d))

        def last_y(d):
            return remote(s1.at[0, lax.rem(y + d, 4)], r2.at[0, d - 1], s2s.at[0, d - 1], s2r.at[0, d - 1], on_y(d))

        for d in (1, 2, 3):
            last_x(d).start()
            last_y(d).start()
        for d in (1, 2, 3):
            last_x(d).wait_recv()
            last_y(d).wait_recv()
        for p, own in ((0, s1[0, y]), (1, s1[1, x])):
            s2[p] = (own.astype(F32) + r2[p, 0].astype(F32) + r2[p, 1].astype(F32) + r2[p, 2].astype(F32)).astype(BF)
        trade = remote(s2.at[other], fin.at[c], fs.at[0], fr.at[0], sib)
        trade.start()
        for i in (2, 3, 4, 5):
            ship(i).wait_recv()
        gain_own = gain[:, pl.ds(pl.multiple_of(z * FB, 128), FB)].astype(F32)
        for b in range(TOK // TB):
            h, r = divmod(b * TB, HALF)
            at = slice(b * TB, (b + 1) * TB)
            hs = slice(r, r + TB)
            one, two = (4, 3) if h == 0 else (2, 5)
            s = cv[right, at, :].astype(F32) + rbuf[one, hs, :].astype(F32) + rbuf[two, hs, :].astype(F32)
            mc = jnp.transpose(jnp.broadcast_to(m[:1, at], (128, TB)))[:, :1]
            inv = inv_b[at, :1]
            result[at, :] = (adv_b[at, :1] * cv[z, at, :].astype(F32) + s * gain_own
                             - packed[at, :].astype(F32) * (inv * mc)).astype(BF)
        trade.wait()
        mine = s2[c]
        got = fin[other]
        low_out[...] = jnp.where(c == 0, mine, got)
        high_out[...] = jnp.where(c == 0, got, mine)
        for i in range(6):
            ship(i).wait_send()
        for i in range(4):
            swap(i).wait_send()
        for d in (1, 2, 3):
            hop_x(d).wait_send()
            hop_y(d).wait_send()
            last_x(d).wait_send()
            last_y(d).wait_send()

    pl.run_scoped(gradients, v((2, 4, 4, 2) + PART), v((2, 4) + PART))
    ring_a.sent()
    ring_b.sent()
    for kind in (note, part_a, part_b):
        for i, o in enumerate(OFFSETS):
            t = peer(o, 1)
            kind(i, t, me, t).wait_send()
    w_pair.wait_send()
    for p, d in hops:
        w_near(p, d).wait_send()
        w_next(p, d).wait_send()
    for d in range(7):
        w_last(d).wait_send()
    for d in (1, 2, 3):
        tell(d).wait_send()


def split_kernel(result, low, high, res, res_q, res_k, res_v, res_o):
    res[...] = result[...]
    res_q[...] = low[:, :QC]
    res_k[...] = low[:, QC:]
    res_v[...] = high[:, :KC]
    res_o[...] = high[:, KC:]


def sds(shape, dtype=BF):
    return jax.ShapeDtypeStruct(shape, dtype)


def params(**kw):
    return pltpu.CompilerParams(vmem_limit_bytes=LIMIT, has_side_effects=True, **kw)


def rope_table():
    i = np.arange(HD // 2, dtype=np.float32)
    frequency = np.float32(ROPE_BASE) ** (-(np.float32(2.0) * i) / np.float32(HD))
    angle = np.arange(128, dtype=np.float32)[:, None] * frequency[None, :]
    c, s = np.cos(angle), np.sin(angle)
    return np.concatenate([c, c, -s, s], axis=1).astype(np.float32)


N_O = len(OFFSETS)
WIDTH = QC + 2 * KC
PART = (112, QC + KC)


def scratch(shape, dtype=BF):
    return pltpu.VMEM(shape, dtype)


def stage(*args):
    return pl.pallas_call(
        stage_kernel, out_shape=(sds((SEQ * SLAB, FA)), sds((SEQ * SLAB, FB - FA)), sds((SEQ * 8, 128), F32)),
        in_specs=[SMEM, VMEM, VMEM, VMEM], out_specs=(VMEM,) * 3, compiler_params=params(),
    )(*args)


def whole(*args):
    v = scratch
    ring = [DMA((6,)), DMA((6,))]
    return pl.pallas_call(
        whole_kernel, out_shape=(sds((TOK, FB)), sds(PART), sds(PART)),
        in_specs=[HBM] * 4 + [VMEM] * 7, out_specs=(VMEM,) * 3,
        scratch_shapes=[
            v((SEQ * SLAB, FB)), v((SEQ * 8, 128), F32),
            v((N_Z, TOK, FB)), v((N_Z, TOK, FB)), v((2,) + PART), v((2, 4, 4, 2) + PART),
            v((8, TOK), F32), v((3, 8, TOK), F32), v((TOK, 128), F32), v((TOK, 2 * HD), F32), v((TOK, 128), F32),
            v((TOK, WIDTH)), v((TOK, QC)), v((TOK, 128), F32), v((TOK, 128), F32), v((8, TOK), F32),
            v((3, 8, TOK), F32), v((6, HALF, FB)), v((4, 4, 2) + PART), v((2, 3, 4) + PART), v((2, 3) + PART),
            v((2,) + PART), v((2,) + PART),
            DMA((4,))] + [DMA((N_O,))] * 6 + ring * 3 + [DMA((4,)), DMA((4,)), DMA((1,)), DMA((1,))]
        + [DMA((2, 3))] * 4 + [DMA((7,))] * 2
        + ring + [DMA((4,))] * 4 + [DMA((2, 3))] * 4 + [DMA((1,))] * 2,
        compiler_params=params(collective_id=0),
    )(*args)


def split(*args):
    return pl.pallas_call(
        split_kernel,
        out_shape=(sds((TOK, FB)), sds((112, QC)), sds((112, KC)), sds((112, KC)), sds((112, QC))),
        in_specs=[VMEM] * 3, out_specs=(VMEM,) * 5, compiler_params=params(),
    )(*args)


def per_device(roll_rows, dest, lengths, clusters, log_prob_grad, gain, w_q, w_k, w_v, w_o_t):
    gain = gain.reshape(1, D)
    send_a, send_b, meta = stage(dest, dest.reshape(1, SEQ), clusters.reshape(1, SEQ), roll_rows)
    return split(*whole(
        send_a, send_b, meta, log_prob_grad, lengths, gain, jnp.asarray(rope_table()), w_q, w_k, w_v, w_o_t))


def solution(mesh):
    in_specs = (
        P("fsdp", None, "tp"), P("fsdp"), P("fsdp", None), P("fsdp"), P("fsdp", "tp"), P(),
        P("fsdp", "tp"), P("fsdp", "tp"), P("fsdp", "tp"), P("fsdp", "tp"),
    )
    out_specs = (P("fsdp", "tp"),) * 5
    return jax.shard_map(per_device, mesh=mesh, in_specs=in_specs, out_specs=out_specs, check_vma=False)
```

time: 205 us -> 198 us (0.966)
  Pallas kernels: 202 us -> 196 us
    pallas_call x4 -> x3, Pallas kernels: 202 us -> 196 us  [the longest x1 188 us: whole(): pl.pallas_call(whole_kernel, out_shape=(sds((TOK, FB)), sds(PART), sds(PA...]
where the time goes in v4:
time: 198 us
  Pallas kernels  196 us (99%)
    pallas_call x1, Pallas kernels, whole(): pl.pallas_call(whole_kernel, out_shape=(sds((TOK, FB)), sds(PART), sds(PA...  188 us
    pallas_call x1, Pallas kernels, stage(): pl.pallas_call(stage_kernel, out_shape=(sds((SEQ * SLAB, FA)), sds((SEQ *...  5.12 us

profile of v4, /device:TPU:1, one launch (start us, length us, event | category | flops | bytes accessed | tf_op | source)
XLA Modules:
  0.0 198.2 jit_solution(10129580578560380010)
XLA Ops:
  0.6 1.3 reshape.21.gain
  1.9 5.1 %shard_map.146 = (bf16[2560,512]{1,0:T(8,128)(2,1)}, bf16[2560,384]{1,0:T(8,128)(2,1)}, f32[256,128]{1,0:T(8,128)}) custom-call(s32[32]{0:T(128)} %dest_s.1, s32[1,32]{1,0:T(1,128)} %bitcast.2, s32[1,32]{1,0:T(1,128)} %bitcast.3, bf16[32,72,896]{2,1,0:T(8,128)(2,1)} %roll.1), custom_call_target="tpu_custom_call" | custom-call | tf_op jit(solution)/shard_map/pallas_call | solution.py:609
  7.1 188.5 %shard_map.147 = (bf16[768,896]{1,0:T(8,128)(2,1)}, bf16[112,640]{1,0:T(8,128)(2,1)}, bf16[112,640]{1,0:T(8,128)(2,1)}) custom-call(bf16[2560,512]{1,0:T(8,128)(2,1)} %get-tuple-element.11.send_a, bf16[2560,384]{1,0:T(8,128)(2,1)} %get-tuple-element.12.send_b, f32[256,128]{1,0:T(8,128)} %get-tuple-element.13.meta, bf16[768,896]{1,0:T(8,128)(2,1)} %cot.1, ...), custom_call_target="tpu_custom_call" | custom-call | tf_op jit(solution)/shard_map/pallas_call | solution.py:618
  195.5 2.7 %shard_map.148 = (bf16[768,896]{1,0:T(8,128)(2,1)}, bf16[112,512]{1,0:T(8,128)(2,1)}, bf16[112,128]{1,0:T(8,128)(2,1)}, bf16[112,128]{1,0:T(8,128)(2,1)}, bf16[112,512]{1,0:T(8,128)(2,1)}) custom-call(bf16[768,896]{1,0:T(8,128)(2,1)} %get-tuple-element.14.result, bf16[112,640]{1,0:T(8,128)(2,1)} %get-tuple-element.15.low, ...), custom_call_target="tpu_custom_call" | custom-call | tf_op jit(solution)/shard_map/pallas_call | solution.py:636

commit v5 on v4

--- a/solution.py
+++ b/solution.py
@@ -105,7 +105,7 @@
     def hand_on(self):
         for i, blk in ((0, self.left), (1, self.right)):
             self.copy(i, blk).wait_recv()
-            self.copy(i + 4, blk, self.dst.at[blk]).start()
+            self.copy(i + 4, blk, self.source(blk)).start()
 
     def near(self):
         self.copy(2, self.left).wait_recv()
@@ -118,8 +118,24 @@
     def sent(self):
         for i in range(4):
             self.copy(i, self.z).wait_send()
-        self.copy(4, self.left, self.dst.at[self.left]).wait_send()
-        self.copy(5, self.right, self.dst.at[self.right]).wait_send()
+        self.copy(4, self.left, self.source(self.left)).wait_send()
+        self.copy(5, self.right, self.source(self.right)).wait_send()
+
+    def source(self, blk):
+        return self.dst.at[blk]
+
+
+class Loop(Ring):
+    def __init__(self, ref, k, to, ss, rs):
+        self.ref, self.z, self.to, self.ss, self.rs = ref, k, to, ss, rs
+        self.right, self.left, self.far = (lax.rem(k + d, 4) for d in (1, 3, 2))
+
+    def copy(self, i, blk, src=None):
+        at = self.ref(blk, (0, 1, 1, 0, 0, 1)[i])
+        return remote(at, at, self.ss.at[i], self.rs.at[i], self.to(1 if i % 2 == 0 else 3))
+
+    def source(self, blk):
+        return None
 
 
 def unstack(v):
@@ -143,8 +159,8 @@
                  arr, meta_in, xv, cv, wsh, wv, sq, sq_all, sqc, rope, pos_b, grads, outs, inv_b, adv_b, dots,
                  dots_all, rbuf, pair, r1, r2, s2, fin,
                  lsem, as_, ar, bs, br, ms, mr, zs, zr, us, ur, vs, vr, qs, qr,
-                 w0s, w0r, w1s, w1r, w2s, w2r, w3s, w3r,
-                 gs, gr, ds_, dr, ps, pr, s1s, s1r, s2s, s2r, fs, fr):
+                 w0s, w0r, w1s, w1r, w3s, w3r, w2s, w2r, w4s, w4r,
+                 gs, gr, ds_, dr, ps, pr, s1s, s1r, hs, hr, s2s, s2r, fs, fr):
     packed = result
     me = lax.axis_index("fsdp")
     z = lax.axis_index("tp")
@@ -212,9 +228,8 @@
     def w_near(p, d):
         return remote(wv.at[c, y, x, p], wv.at[c, y, x, p], w1s.at[p, d - 1], w1r.at[p, d - 1], on_y(d) if p else on_x(d))
 
-    def w_next(p, d):
-        blk = wv.at[c, :, x, 1] if p else wv.at[c, y, :, 0]
-        return remote(blk, blk, w2s.at[p, d - 1], w2r.at[p, d - 1], on_x(d) if p else on_y(d))
+    loops = [Loop(lambda k, h: wv.at[c, k, pl.ds(2 * h, 2), 0], y, on_y, w2s, w2r),
+             Loop(lambda k, h: wv.at[c, pl.ds(2 * h, 2), k, 1], x, on_x, w4s, w4r)]
 
     def w_last(d):
         if d < 3:
@@ -294,8 +309,8 @@
         mine[1].wait()
         for p, d in hops:
             w_near(p, d).wait_recv()
-        for p, d in hops:
-            w_next(p, d).start()
+        for loop in loops:
+            loop.start()
         pack(FA, FB)
         ring_b.start()
     pl.run_scoped(packing, scratch((TOK, SEQ * SLAB)))
@@ -308,6 +323,8 @@
 
     for d in (1, 2, 3):
         tell(d).start()
+    for loop in loops:
+        loop.hand_on()
     ring_b.hand_on()
     ring_a.near()
     ring_a.end()
@@ -316,8 +333,9 @@
     inv_t = lax.rsqrt((sq[...] + sq_all[0] + sq_all[1] + sq_all[2]) * (1.0 / D) + NORM_EPSILON)
     for b in range(TOK // TB):
         inv_b[b * TB:(b + 1) * TB, :] = jnp.transpose(jnp.broadcast_to(inv_t[:1, b * TB:(b + 1) * TB], (128, TB)))
-    for p, d in hops:
-        w_next(p, d).wait_recv()
+    for loop in loops:
+        loop.near()
+        loop.end()
     for d in range(7):
         w_last(d).start()
     for d in range(7):
@@ -404,7 +422,7 @@
                 outs[at, col] = (o[:, col] * adv_b[at, :]).astype(BF)
             return carry
 
-        lax.fori_loop(0, TOK // TB, attend, 0)
+        lax.fori_loop(0, TOK // TB, attend, 0, unroll=True)
 
         def finish(b, carry):
             at = pl.ds(pl.multiple_of(b * TB, TB), TB)
@@ -465,37 +483,47 @@
             swap(i).start()
             return carry
 
-        lax.fori_loop(0, 2, terms, 0)
+        def hop_y(d):
+            return remote(dw.at[c, lax.rem(y + d, 4), :, 1], r1.at[1, d - 1], s1s.at[1, d - 1], s1r.at[1, d - 1], on_y(d))
+
+        def hop_x(i, d):
+            b = lax.rem(y + 1 + i, 4)
+            return remote(dw.at[c, b, lax.rem(x + d, 4), 0], r1.at[0, d - 1, b], hs.at[i, d - 1], hr.at[i, d - 1], on_x(d))
+
+        def chip_sum(i, carry):
+            b = lax.rem(y + 1 + i, 4)
+            swap(i).wait_recv()
+            for j in range(4):
+                dw[c, b, j] = (dw[c, b, j].astype(F32) + pair[b, j].astype(F32)).astype(BF)
+
+            def along_y():
+                hop_y(i + 1).start()
+
+            if not isinstance(i, int):
+                pl.when(i < 3)(along_y)
+
+            for d in (1, 2, 3):
+                hop_x(i, d).start()
+
+        def step(i, carry):
+            terms(i, carry)
+
+            @pl.when(i > 0)
+            def _():
+                chip_sum(i - 1, carry)
+
+            return carry
+
+        lax.fori_loop(0, 2, step, 0)
         first(2, 1, 1)
         first(3, 2, 0)
-        lax.fori_loop(2, 4, terms, 0)
+        lax.fori_loop(2, 4, step, 0)
+        chip_sum(3, 0)
         for i, w in ((4, 1), (5, 2)):
             a = share(w, i % 2)
             ship(i - 4).wait_recv()
             arr[i * HALF:(i + 1) * HALF, :] = (a + rbuf[i - 4].astype(F32)).astype(BF)
             ship(i).start()
-
-        def hop_y(d):
-            return remote(dw.at[c, lax.rem(y + d, 4), :, 1], r1.at[1, d - 1], s1s.at[1, d - 1], s1r.at[1, d - 1], on_y(d))
-
-        def hop_x(d):
-            return remote(dw.at[c, :, lax.rem(x + d, 4), 0], r1.at[0, d - 1], s1s.at[0, d - 1], s1r.at[0, d - 1], on_x(d))
-
-        def chip_sum(i, carry):
-            b = lax.rem(y + 1 + i, 4)
-            swap(i).wait_recv()
-            for j in range(4):
-                dw[c, b, j] = (dw[c, b, j].astype(F32) + pair[b, j].astype(F32)).astype(BF)
-
-            @pl.when(i < 3)
-            def _():
-                hop_y(i + 1).start()
-
-            return carry
-
-        lax.fori_loop(0, 4, chip_sum, 0)
-        for d in (1, 2, 3):
-            hop_x(d).start()
         for h in range(2):
             cv[right, h * HALF:(h + 1) * HALF, :] = share(3, h).astype(BF)
         for d in (1, 2, 3):
@@ -504,7 +532,8 @@
 
         for d in (1, 2, 3):
             hop_y(d).wait_recv()
-            hop_x(d).wait_recv()
+            for i in range(4):
+                hop_x(i, d).wait_recv()
         for j in range(4):
             s1[1, j] = (dw[c, y, j, 1].astype(F32) + r1[1, 0, j].astype(F32) + r1[1, 1, j].astype(F32)
                         + r1[1, 2, j].astype(F32)).astype(BF)
@@ -533,9 +562,9 @@
         for b in range(TOK // TB):
             h, r = divmod(b * TB, HALF)
             at = slice(b * TB, (b + 1) * TB)
-            hs = slice(r, r + TB)
+            rows = slice(r, r + TB)
             one, two = (4, 3) if h == 0 else (2, 5)
-            s = cv[right, at, :].astype(F32) + rbuf[one, hs, :].astype(F32) + rbuf[two, hs, :].astype(F32)
+            s = cv[right, at, :].astype(F32) + rbuf[one, rows, :].astype(F32) + rbuf[two, rows, :].astype(F32)
             mc = jnp.transpose(jnp.broadcast_to(m[:1, at], (128, TB)))[:, :1]
             inv = inv_b[at, :1]
             result[at, :] = (adv_b[at, :1] * cv[z, at, :].astype(F32) + s * gain_own
@@ -550,7 +579,8 @@
         for i in range(4):
             swap(i).wait_send()
         for d in (1, 2, 3):
-            hop_x(d).wait_send()
+            for i in range(4):
+                hop_x(i, d).wait_send()
             hop_y(d).wait_send()
             last_x(d).wait_send()
             last_y(d).wait_send()
@@ -565,7 +595,8 @@
     w_pair.wait_send()
     for p, d in hops:
         w_near(p, d).wait_send()
-        w_next(p, d).wait_send()
+    for loop in loops:
+        loop.sent()
     for d in range(7):
         w_last(d).wait_send()
     for d in (1, 2, 3):
@@ -626,8 +657,8 @@
             v((3, 8, TOK), F32), v((6, HALF, FB)), v((4, 4, 2) + PART), v((2, 3, 4) + PART), v((2, 3) + PART),
             v((2,) + PART), v((2,) + PART),
             DMA((4,))] + [DMA((N_O,))] * 6 + ring * 3 + [DMA((4,)), DMA((4,)), DMA((1,)), DMA((1,))]
-        + [DMA((2, 3))] * 4 + [DMA((7,))] * 2
-        + ring + [DMA((4,))] * 4 + [DMA((2, 3))] * 4 + [DMA((1,))] * 2,
+        + [DMA((2, 3))] * 2 + [DMA((7,))] * 2 + ring * 2
+        + ring + [DMA((4,))] * 4 + [DMA((2, 3))] * 2 + [DMA((4, 3))] * 2 + [DMA((2, 3))] * 2 + [DMA((1,))] * 2,
         compiler_params=params(collective_id=0),
     )(*args)
 

time: 198 us -> 186 us (0.939)
  Pallas kernels: 196 us -> 184 us
    pallas_call x1, Pallas kernels: 188 us -> 176 us  [whole(): pl.pallas_call(whole_kernel, out_shape=(sds((TOK, FB)), sds(PART), sds(PA...]
where the time goes in v5:
time: 186 us
  Pallas kernels  184 us (99%)
    pallas_call x1, Pallas kernels, whole(): pl.pallas_call(whole_kernel, out_shape=(sds((TOK, FB)), sds(PART), sds(PA...  176 us
    pallas_call x1, Pallas kernels, stage(): pl.pallas_call(stage_kernel, out_shape=(sds((SEQ * SLAB, FA)), sds((SEQ *...  5.12 us

profile of v5, /device:TPU:1, one launch (start us, length us, event | category | flops | bytes accessed | tf_op | source)
XLA Modules:
  0.0 185.5 jit_solution(8914762937784924142)
XLA Ops:
  0.6 1.3 reshape.21.gain
  1.9 5.1 %shard_map.146 = (bf16[2560,512]{1,0:T(8,128)(2,1)}, bf16[2560,384]{1,0:T(8,128)(2,1)}, f32[256,128]{1,0:T(8,128)}) custom-call(s32[32]{0:T(128)} %dest_s.1, s32[1,32]{1,0:T(1,128)} %bitcast.2, s32[1,32]{1,0:T(1,128)} %bitcast.3, bf16[32,72,896]{2,1,0:T(8,128)(2,1)} %roll.1), custom_call_target="tpu_custom_call" | custom-call | tf_op jit(solution)/shard_map/pallas_call | solution.py:640
  7.1 175.8 %shard_map.147 = (bf16[768,896]{1,0:T(8,128)(2,1)}, bf16[112,640]{1,0:T(8,128)(2,1)}, bf16[112,640]{1,0:T(8,128)(2,1)}) custom-call(bf16[2560,512]{1,0:T(8,128)(2,1)} %get-tuple-element.11.send_a, bf16[2560,384]{1,0:T(8,128)(2,1)} %get-tuple-element.12.send_b, f32[256,128]{1,0:T(8,128)} %get-tuple-element.13.meta, bf16[768,896]{1,0:T(8,128)(2,1)} %cot.1, ...), custom_call_target="tpu_custom_call" | custom-call | tf_op jit(solution)/shard_map/pallas_call | solution.py:649
  182.9 2.7 %shard_map.148 = (bf16[768,896]{1,0:T(8,128)(2,1)}, bf16[112,512]{1,0:T(8,128)(2,1)}, bf16[112,128]{1,0:T(8,128)(2,1)}, bf16[112,128]{1,0:T(8,128)(2,1)}, bf16[112,512]{1,0:T(8,128)(2,1)}) custom-call(bf16[768,896]{1,0:T(8,128)(2,1)} %get-tuple-element.14.result, bf16[112,640]{1,0:T(8,128)(2,1)} %get-tuple-element.15.low, ...), custom_call_target="tpu_custom_call" | custom-call | tf_op jit(solution)/shard_map/pallas_call | solution.py:667

commit v6 on v5

--- a/solution.py
+++ b/solution.py
@@ -186,6 +186,10 @@
         pl.semaphore_signal(barrier, inc=1, device_id={"tp": lax.rem(z + d, N_Z)}, device_id_type=MESH)
     pl.semaphore_wait(barrier, len(OFFSETS) + 3)
 
+    def own_gain():
+        g = gain[...].astype(F32).reshape(1, D)
+        return sum(jnp.where(z == k, g[:, k * FB:(k + 1) * FB], 0.0) for k in range(N_Z))
+
     ring_c = Ring(cot, cv, pl.ds(0, FB), z, zs, zr)
     ring_a = Ring(xv.at[z], xv, pl.ds(0, FA), z, us, ur)
     ring_b = Ring(xv.at[z], xv, pl.ds(FA, FB - FA), z, vs, vr)
@@ -246,7 +250,7 @@
         w_near(p, d).start()
 
     lens = diagonal(len_r[...].astype(F32), SEQ)
-    gain_own = gain[:, pl.ds(pl.multiple_of(z * FB, 128), FB)].astype(F32)
+    gain_own = own_gain()
     lane = iota((SEQ, 128), 1)
     sub = iota((SEQ, 128), 0)
     ends = jnp.sum(jnp.where(sub <= lane, lens, 0.0), axis=0, keepdims=True)
@@ -338,6 +342,13 @@
         loop.end()
     for d in range(7):
         w_last(d).start()
+    for kind in (note, part_a, part_b):
+        for i, o in enumerate(OFFSETS):
+            t = peer(o, 1)
+            kind(i, t, me, t).wait_send()
+    w_pair.wait_send()
+    for p, d in hops:
+        w_near(p, d).wait_send()
     for d in range(7):
         w_last(d).wait_recv()
 
@@ -558,7 +569,7 @@
         trade.start()
         for i in (2, 3, 4, 5):
             ship(i).wait_recv()
-        gain_own = gain[:, pl.ds(pl.multiple_of(z * FB, 128), FB)].astype(F32)
+        gain_own = own_gain()
         for b in range(TOK // TB):
             h, r = divmod(b * TB, HALF)
             at = slice(b * TB, (b + 1) * TB)
@@ -588,13 +599,6 @@
     pl.run_scoped(gradients, v((2, 4, 4, 2) + PART), v((2, 4) + PART))
     ring_a.sent()
     ring_b.sent()
-    for kind in (note, part_a, part_b):
-        for i, o in enumerate(OFFSETS):
-            t = peer(o, 1)
-            kind(i, t, me, t).wait_send()
-    w_pair.wait_send()
-    for p, d in hops:
-        w_near(p, d).wait_send()
     for loop in loops:
         loop.sent()
     for d in range(7):
@@ -672,7 +676,6 @@
 
 
 def per_device(roll_rows, dest, lengths, clusters, log_prob_grad, gain, w_q, w_k, w_v, w_o_t):
-    gain = gain.reshape(1, D)
     send_a, send_b, meta = stage(dest, dest.reshape(1, SEQ), clusters.reshape(1, SEQ), roll_rows)
     return split(*whole(
         send_a, send_b, meta, log_prob_grad, lengths, gain, jnp.asarray(rope_table()), w_q, w_k, w_v, w_o_t))

time: 186 us -> 184 us (0.989)
  no operation moved by 1% of the time
where the time goes in v6:
time: 184 us
  Pallas kernels  183 us (99%)
    pallas_call x1, Pallas kernels, whole(): pl.pallas_call(whole_kernel, out_shape=(sds((TOK, FB)), sds(PART), sds(PA...  176 us
    pallas_call x1, Pallas kernels, stage(): pl.pallas_call(stage_kernel, out_shape=(sds((SEQ * SLAB, FA)), sds((SEQ *...  5.12 us

profile of v6, /device:TPU:1, one launch (start us, length us, event | category | flops | bytes accessed | tf_op | source)
XLA Modules:
  0.0 184.0 jit_solution(15470506032127273862)
XLA Ops:
  0.6 5.1 %shard_map.146 = (bf16[2560,512]{1,0:T(8,128)(2,1)}, bf16[2560,384]{1,0:T(8,128)(2,1)}, f32[256,128]{1,0:T(8,128)}) custom-call(s32[32]{0:T(128)} %dest_s.1, s32[1,32]{1,0:T(1,128)} %bitcast.2, s32[1,32]{1,0:T(1,128)} %bitcast.3, bf16[32,72,896]{2,1,0:T(8,128)(2,1)} %roll.1), custom_call_target="tpu_custom_call" | custom-call | tf_op jit(solution)/shard_map/pallas_call | solution.py:644
  5.7 175.6 %shard_map.147 = (bf16[768,896]{1,0:T(8,128)(2,1)}, bf16[112,640]{1,0:T(8,128)(2,1)}, bf16[112,640]{1,0:T(8,128)(2,1)}) custom-call(bf16[2560,512]{1,0:T(8,128)(2,1)} %get-tuple-element.11.send_a, bf16[2560,384]{1,0:T(8,128)(2,1)} %get-tuple-element.12.send_b, f32[256,128]{1,0:T(8,128)} %get-tuple-element.13.meta, bf16[768,896]{1,0:T(8,128)(2,1)} %cot.1, ...), custom_call_target="tpu_custom_call" | custom-call | tf_op jit(solution)/shard_map/pallas_call | solution.py:653
  181.4 2.7 %shard_map.148 = (bf16[768,896]{1,0:T(8,128)(2,1)}, bf16[112,512]{1,0:T(8,128)(2,1)}, bf16[112,128]{1,0:T(8,128)(2,1)}, bf16[112,128]{1,0:T(8,128)(2,1)}, bf16[112,512]{1,0:T(8,128)(2,1)}) custom-call(bf16[768,896]{1,0:T(8,128)(2,1)} %get-tuple-element.14.result, bf16[112,640]{1,0:T(8,128)(2,1)} %get-tuple-element.15.low, ...), custom_call_target="tpu_custom_call" | custom-call | tf_op jit(solution)/shard_map/pallas_call | solution.py:671
